TPU v7x, 32 devices: a whole 2x2x4 slice. The times are simulated.
32 devices in a mesh: batch: 4 (over y, x), seq: 8 (over z, core).
Axes of the slice: x: 2, y: 2, z: 4, core: 2. Of those that a mesh axis runs over, the one named last changes fastest.
Arguments:
- tokens: bfloat16 [32, 2048, 576], P('batch', 'seq'), may hold values from -6 to 6
- lengths: int32 [32], P('batch'), may hold values from 512 to 2048, as said below
- gain_attn: float32 [576], replicated, may hold values from 0.5 to 1.5
- w_query: bfloat16 [576, 576], replicated, may hold values from -0.25 to 0.25
- w_key: bfloat16 [576, 192], replicated, may hold values from -0.25 to 0.25
- w_value: bfloat16 [576, 192], replicated, may hold values from -0.25 to 0.25
- w_out: bfloat16 [576, 576], replicated, may hold values from -3 to 3
- gain_mlp: float32 [576], replicated, may hold values from 0.5 to 1.5
- w_gate: bfloat16 [576, 1536], replicated, may hold values from -0.25 to 0.25
- w_up: bfloat16 [576, 1536], replicated, may hold values from -0.25 to 0.25
- w_down: bfloat16 [1536, 576], replicated, may hold values from -0.15625 to 0.15625
- cotangent: bfloat16 [32, 2048, 576], P('batch', 'seq'), may hold values from -6 to 6
Outputs:
- layer_out: bfloat16 [32, 2048, 576], P('batch', 'seq')
- grad_tokens: bfloat16 [32, 2048, 576], P('batch', 'seq')
- grad_gain_attn: float32 [576], replicated
- grad_w_query: float32 [576, 576], replicated
- grad_w_key: float32 [576, 192], replicated
- grad_w_value: float32 [576, 192], replicated
- grad_w_out: float32 [576, 576], replicated
- grad_gain_mlp: float32 [576], replicated
- grad_w_gate: float32 [576, 1536], replicated
- grad_w_up: float32 [576, 1536], replicated
- grad_w_down: float32 [1536, 576], replicated
Inputs may be any that keep to these rules, and one draw needn't show every extreme that they name: `lengths`: in each aligned block of 8 row slots one slot has length 2048 and another 2048 // 4.
All inputs are finite; a program needn't handle non-finite values.
Results may differ from a plain program's by a relative error of at most 0.015.
Values may be sent and summed in bfloat16 or wider, within the bound.
No kernel may reach another device: no remote copies, remote signals or barrier semaphores. Data moves between devices by JAX's collectives and lax.ppermute only.
A program may use at most 320 MiB of HBM per device.

v0:
```python
import jax
import jax.numpy as jnp
from jax import lax
from jax.sharding import PartitionSpec as P

H = 9
KVH = 3
HD = 64


EPSILON = 1e-05
ROPE_BASE = 10000.0
MASKED_SCORE = -1e30


def rope_tables(positions):
    freqs = ROPE_BASE ** (-(jnp.arange(HD // 2, dtype=jnp.float32) * 2.0) / HD)
    phases = positions[:, None] * freqs[None, :]
    phases = jnp.concatenate([phases, phases], axis=-1)
    return (jnp.cos(phases)[:, None, :], jnp.sin(phases)[:, None, :])


def rotate(vectors, cosine_table, sine_table):
    half_size = vectors.shape[-1] // 2
    turned = jnp.concatenate([-vectors[..., half_size:], vectors[..., :half_size]], axis=-1)
    return vectors * cosine_table + turned * sine_table


def rotate_back(gradient, cosine_table, sine_table):
    half_size = gradient.shape[-1] // 2
    scaled = gradient * sine_table
    turned = jnp.concatenate([scaled[..., half_size:], -scaled[..., :half_size]], axis=-1)
    return gradient * cosine_table + turned


def rms_scale(vectors):
    return lax.rsqrt(jnp.mean(vectors * vectors, axis=-1, keepdims=True) + EPSILON)


def norm_back(grad_normed, normed, inv_scale):
    return inv_scale * (
        grad_normed - normed * jnp.mean(grad_normed * normed, axis=-1, keepdims=True)
    )


def project(vectors, matrix):
    return jnp.einsum("rtd,de->rte", vectors, matrix, preferred_element_type=jnp.float32)


def project_back(gradient, matrix):
    return jnp.einsum("rte,de->rtd", gradient, matrix, preferred_element_type=jnp.float32)


def weight_grad(vectors, gradient):
    return jnp.einsum("rtd,rte->de", vectors, gradient, preferred_element_type=jnp.float32)


def body(
    tokens,
    lengths,
    gain_attn,
    w_query,
    w_key,
    w_value,
    w_out,
    gain_mlp,
    w_gate,
    w_up,
    w_down,
    cotangent,
):
    row_count, local_len, model_width = tokens.shape
    group_size = H // KVH
    kv_width = KVH * HD
    key_len = local_len * lax.axis_size("seq")
    score_scale = HD ** (-0.5)
    start = lax.axis_index("seq") * local_len
    positions = start + jnp.arange(local_len, dtype=jnp.int32)
    cosine_table, sine_table = rope_tables(positions.astype(jnp.float32))
    valid = (positions[None, :] < lengths[:, None]).astype(jnp.float32)[..., None]
    key_positions = jnp.arange(key_len, dtype=jnp.int32)
    allowed_keys = (key_positions[None, None, :] <= positions[None, :, None]) & (
        key_positions[None, None, :] < lengths[:, None, None]
    )
    group_rows = min(row_count, max(1, 512 // local_len))
    group_count = row_count // group_rows

    def regroup(array):
        return array.reshape((group_count, group_rows) + array.shape[1:])

    inputs = tokens.astype(jnp.float32)
    attn_scale = rms_scale(inputs)
    normed_attn = inputs * attn_scale
    attn_in = (normed_attn * gain_attn).astype(jnp.bfloat16)
    query_pre = project(attn_in, w_query)
    key_pre = project(attn_in, w_key)
    value_rows = project(attn_in, w_value).astype(jnp.bfloat16)
    queries = rotate(
        query_pre.reshape(row_count, local_len, H, HD), cosine_table, sine_table
    ).astype(jnp.bfloat16)
    queries = queries.reshape(row_count, local_len, KVH, group_size, HD)
    key_rows = rotate(
        key_pre.reshape(row_count, local_len, KVH, HD), cosine_table, sine_table
    ).astype(jnp.bfloat16)
    key_rows = key_rows.reshape(row_count, local_len, kv_width)
    key_whole, value_whole = (
        lax.all_gather(key_rows, "seq", axis=1, tiled=True),
        lax.all_gather(value_rows, "seq", axis=1, tiled=True),
    )

    def scores_of(query_block, key_block, allowed_block):
        key_heads = key_block.reshape(key_block.shape[0], key_len, KVH, HD)
        raw_scores = (
            jnp.einsum(
                "rqkgd,rskd->rkgqs", query_block, key_heads, preferred_element_type=jnp.float32
            )
            * score_scale
        )
        return jnp.where(allowed_block[:, None, None, :, :], raw_scores, MASKED_SCORE)

    def forward_block(pieces):
        query_block, key_block, value_block, allowed_block = pieces
        masked = scores_of(query_block, key_block, allowed_block)
        row_peak = jnp.max(masked, axis=-1, keepdims=True)
        weights = jnp.exp(masked - row_peak)
        row_total = jnp.sum(weights, axis=-1, keepdims=True)
        probs = (weights / row_total).astype(jnp.bfloat16)
        value_heads = value_block.reshape(value_block.shape[0], key_len, KVH, HD)
        mixed_block = jnp.einsum(
            "rkgqs,rskd->rqkgd", probs, value_heads, preferred_element_type=jnp.float32
        )
        mixed_block = mixed_block.astype(jnp.bfloat16).reshape(
            value_block.shape[0], local_len, H * HD
        )
        return (mixed_block, row_peak + jnp.log(row_total))

    mixed, log_totals = lax.map(
        forward_block,
        (regroup(queries), regroup(key_whole), regroup(value_whole), regroup(allowed_keys)),
    )
    mixed = mixed.reshape(row_count, local_len, H * HD)
    resid = inputs + project(mixed, w_out)
    mlp_scale = rms_scale(resid)
    normed_mlp = resid * mlp_scale
    mlp_in = (normed_mlp * gain_mlp).astype(jnp.bfloat16)
    gate_proj = project(mlp_in, w_gate)
    up_proj = project(mlp_in, w_up)
    sigmoid_gate = jax.nn.sigmoid(gate_proj)
    activated = gate_proj * sigmoid_gate
    hidden = (activated * up_proj).astype(jnp.bfloat16)
    layer_out = ((resid + project(hidden, w_down)) * valid).astype(jnp.bfloat16)
    grad_out = cotangent.astype(jnp.float32) * valid
    grad_out_low = grad_out.astype(jnp.bfloat16)
    grad_down = weight_grad(hidden, grad_out_low)
    grad_hidden = project_back(grad_out_low, w_down)
    grad_gate_pre = (
        grad_hidden * up_proj * sigmoid_gate * (1.0 + gate_proj * (1.0 - sigmoid_gate))
    ).astype(jnp.bfloat16)
    grad_up_pre = (grad_hidden * activated).astype(jnp.bfloat16)
    grad_gate = weight_grad(mlp_in, grad_gate_pre)
    grad_up = weight_grad(mlp_in, grad_up_pre)
    grad_mlp_in = project_back(grad_gate_pre, w_gate) + project_back(grad_up_pre, w_up)
    grad_gain_mlp = jnp.sum(grad_mlp_in * normed_mlp, axis=(0, 1))
    grad_resid = grad_out + norm_back(grad_mlp_in * gain_mlp, normed_mlp, mlp_scale)
    grad_attn = grad_resid.astype(jnp.bfloat16)
    grad_out_proj = weight_grad(mixed, grad_attn)
    grad_mixed = project_back(grad_attn, w_out).astype(jnp.bfloat16)
    key_back, value_back = (key_whole, value_whole)

    def backward_block(pieces):
        query_block, key_block, value_block, allowed_block, log_block, grad_block = pieces
        masked = scores_of(query_block, key_block, allowed_block)
        probs = jnp.exp(masked - log_block)
        block_rows = query_block.shape[0]
        value_heads = value_block.reshape(block_rows, key_len, KVH, HD)
        key_heads = key_block.reshape(block_rows, key_len, KVH, HD)
        grad_heads = grad_block.reshape(block_rows, local_len, KVH, group_size, HD)
        grad_probs = jnp.einsum(
            "rqkgd,rskd->rkgqs", grad_heads, value_heads, preferred_element_type=jnp.float32
        )
        row_inner = jnp.sum(probs * grad_probs, axis=-1, keepdims=True)
        grad_scores = (probs * (grad_probs - row_inner)).astype(jnp.bfloat16)
        grad_query = (
            jnp.einsum(
                "rkgqs,rskd->rqkgd", grad_scores, key_heads, preferred_element_type=jnp.float32
            )
            * score_scale
        )
        grad_key = (
            jnp.einsum(
                "rkgqs,rqkgd->rskd", grad_scores, query_block, preferred_element_type=jnp.float32
            )
            * score_scale
        )
        grad_value = jnp.einsum(
            "rkgqs,rqkgd->rskd",
            probs.astype(jnp.bfloat16),
            grad_heads,
            preferred_element_type=jnp.float32,
        )
        return (
            grad_query.reshape(block_rows, local_len, H * HD),
            grad_key.reshape(block_rows, key_len, kv_width),
            grad_value.reshape(block_rows, key_len, kv_width),
        )

    grad_query, grad_key, grad_value = lax.map(
        backward_block,
        (
            regroup(queries),
            regroup(key_back),
            regroup(value_back),
            regroup(allowed_keys),
            log_totals,
            regroup(grad_mixed),
        ),
    )
    grad_key = grad_key.reshape(row_count, key_len, kv_width)
    grad_value = grad_value.reshape(row_count, key_len, kv_width)
    grad_key, grad_value = (
        lax.psum_scatter(
            grad_key.astype(jnp.bfloat16), "seq", scatter_dimension=1, tiled=True
        ).astype(jnp.float32),
        lax.psum_scatter(
            grad_value.astype(jnp.bfloat16), "seq", scatter_dimension=1, tiled=True
        ).astype(jnp.float32),
    )
    grad_query_pre = rotate_back(
        grad_query.reshape(row_count, local_len, H, HD), cosine_table, sine_table
    )
    grad_query_pre = grad_query_pre.astype(jnp.bfloat16).reshape(row_count, local_len, H * HD)
    grad_key_pre = rotate_back(
        grad_key.reshape(row_count, local_len, KVH, HD), cosine_table, sine_table
    )
    grad_key_pre = grad_key_pre.astype(jnp.bfloat16).reshape(row_count, local_len, kv_width)
    grad_value_pre = grad_value.astype(jnp.bfloat16)
    grad_query_w = weight_grad(attn_in, grad_query_pre)
    grad_key_w = weight_grad(attn_in, grad_key_pre)
    grad_value_w = weight_grad(attn_in, grad_value_pre)
    grad_attn_in = (
        project_back(grad_query_pre, w_query)
        + project_back(grad_key_pre, w_key)
        + project_back(grad_value_pre, w_value)
    )
    grad_gain_attn = jnp.sum(grad_attn_in * normed_attn, axis=(0, 1))
    grad_tokens = (
        grad_resid + norm_back(grad_attn_in * gain_attn, normed_attn, attn_scale)
    ).astype(jnp.bfloat16)
    (
        grad_gain_attn,
        grad_query_w,
        grad_key_w,
        grad_value_w,
        grad_out_proj,
        grad_gain_mlp,
        grad_gate,
        grad_up,
        grad_down,
    ) = lax.psum(
        (
            grad_gain_attn,
            grad_query_w,
            grad_key_w,
            grad_value_w,
            grad_out_proj,
            grad_gain_mlp,
            grad_gate,
            grad_up,
            grad_down,
        ),
        ("batch", "seq"),
    )
    return (
        layer_out,
        grad_tokens,
        grad_gain_attn,
        grad_query_w,
        grad_key_w,
        grad_value_w,
        grad_out_proj,
        grad_gain_mlp,
        grad_gate,
        grad_up,
        grad_down,
    )


def solution(mesh):
    in_specs = (
        P("batch", "seq", None),
        P("batch"),
        P(),
        P(),
        P(),
        P(),
        P(),
        P(),
        P(),
        P(),
        P(),
        P("batch", "seq", None),
    )
    out_specs = (
        P("batch", "seq", None),
        P("batch", "seq", None),
        P(),
        P(),
        P(),
        P(),
        P(),
        P(),
        P(),
        P(),
        P(),
    )
    return jax.shard_map(body, mesh=mesh, in_specs=in_specs, out_specs=out_specs, check_vma=False)
```

profile of v0, /device:TPU:0, one launch (start us, length us, event | category | flops | bytes accessed | tf_op | source)
XLA Modules:
  0.0 1341.2 jit_solution(2462438150905477458)
XLA Ops:
  32.1 48.9 %all-gather.3.cloned.1.call-done = bf16[8,2048,192]{1,2,0:T(8,128)(2,1)} async-done(((bf16[8,256,192]{1,2,0:T(8,128)(2,1)}), bf16[8,2048,192]{1,2,0:T(8,128)(2,1)}) %all-gather.3.cloned.1.call-update) | async-done | bytes 6291472 | tf_op jit(solution)/shard_map/all_gather | solution.py:108
  81.0 65.6 %all-gather.5.cloned.1.call-done = bf16[8,2048,192]{1,2,0:T(8,128)(2,1)} async-done(((bf16[8,256,192]{1,2,0:T(8,128)(2,1)}), bf16[8,2048,192]{1,2,0:T(8,128)(2,1)}) %all-gather.5.cloned.1.call-update) | async-done | bytes 6291472 | tf_op jit(solution)/shard_map/all_gather | solution.py:107
  146.6 222.3 %while.26 = (s32[]{:T(128)}, bf16[4,2,256,576]{2,3,1,0:T(8,128)(2,1)}, f32[4,2,3,3,256,1]{4,3,2,1,5,0:T(4,128)S(1)}, bf16[4,2,2048,192]{2,3,1,0:T(8,128)(2,1)}, ...) while((s32[]{:T(128)}, ...), condition=%wide.region_4.5_spmd, body=%wide.region_1.4_spmd.sunk | while | flops 2529455616 | bytes 130451560 | solution.py:137
  151.5 16.0 %fusion.133 = (f32[2,3,3,256]{3,2,1,0:T(4,128)S(1)}, f32[2,3,2048,256,3]{3,2,4,1,0:T(8,128)}) fusion(pred[2,256,2048]{1,2,0:T(8,128)(4,1)S(1)} %dynamic-slice_bitcast_fusion.6, bf16[2,2048,3,64,1]{1,3,4,2,0:T(8,128)(2,1)S(1)} %bitcast.281, bf16[4,2,256,3,3,64]{2,5,4,3,1,0:T(8,128)(2,1)} %get-tuple-element.324, s32[]{:T(128)S(6)} %copy.57), kind=kOutput, calls=%fused_computation.4.clone.1 | convolution fusion | flops 1236266496 | bytes 40978436 | tf_op jit(solution)/shard_map/while/body/eval_jaxpr/rqkgd,rskd->rkgqs/dot_general | solution.py:114
  167.5 16.3 %fusion.134 = f32[2,3,3,256]{3,2,1,0:T(4,128)S(1)} fusion(f32[2,3,2048,256,3]{3,2,4,1,0:T(8,128)} %get-tuple-element.286, f32[2,3,3,256]{3,2,1,0:T(4,128)S(1)} %get-tuple-element.287, pred[2,256,2048]{1,2,0:T(8,128)(4,1)S(1)} %dynamic-slice_bitcast_fusion.6), kind=kLoop, calls=%fused_computation.3.clone.1 | loop fusion | flops 37744128 | bytes 38834176 | tf_op jit(solution)/shard_map/while/body/eval_jaxpr/reduce_sum | solution.py:126
  183.8 17.3 %fusion.135 = bf16[2,3,64,3,256]{4,2,3,1,0:T(8,128)(2,1)S(1)} fusion(bf16[2,2048,3,64,1]{1,3,4,2,0:T(8,128)(2,1)} %bitcast.290, f32[2,3,2048,256,3]{3,2,4,1,0:T(8,128)} %get-tuple-element.286, f32[2,3,3,256]{3,2,1,0:T(4,128)S(1)} %fusion.134, f32[2,3,3,256]{3,2,1,0:T(4,128)S(1)} %get-tuple-element.287, ...), kind=kOutput, calls=%fused_computation.7.clone.1 | convolution fusion | flops 1255440384 | bytes 40996864 | tf_op jit(solution)/shard_map/while/body/eval_jaxpr/rkgqs,rskd->rqkgd/dot_general | solution.py:129
  207.0 16.0 %fusion.133 = (f32[2,3,3,256]{3,2,1,0:T(4,128)S(1)}, f32[2,3,2048,256,3]{3,2,4,1,0:T(8,128)}) fusion(pred[2,256,2048]{1,2,0:T(8,128)(4,1)S(1)} %dynamic-slice_bitcast_fusion.6, bf16[2,2048,3,64,1]{1,3,4,2,0:T(8,128)(2,1)S(1)} %bitcast.281, bf16[4,2,256,3,3,64]{2,5,4,3,1,0:T(8,128)(2,1)} %get-tuple-element.324, s32[]{:T(128)S(6)} %copy.57), kind=kOutput, calls=%fused_computation.4.clone.1 | convolution fusion | flops 1236266496 | bytes 40978436 | tf_op jit(solution)/shard_map/while/body/eval_jaxpr/rqkgd,rskd->rkgqs/dot_general | solution.py:114
  223.0 16.3 %fusion.134 = f32[2,3,3,256]{3,2,1,0:T(4,128)S(1)} fusion(f32[2,3,2048,256,3]{3,2,4,1,0:T(8,128)} %get-tuple-element.286, f32[2,3,3,256]{3,2,1,0:T(4,128)S(1)} %get-tuple-element.287, pred[2,256,2048]{1,2,0:T(8,128)(4,1)S(1)} %dynamic-slice_bitcast_fusion.6), kind=kLoop, calls=%fused_computation.3.clone.1 | loop fusion | flops 37744128 | bytes 38834176 | tf_op jit(solution)/shard_map/while/body/eval_jaxpr/reduce_sum | solution.py:126
  239.3 17.3 %fusion.135 = bf16[2,3,64,3,256]{4,2,3,1,0:T(8,128)(2,1)S(1)} fusion(bf16[2,2048,3,64,1]{1,3,4,2,0:T(8,128)(2,1)} %bitcast.290, f32[2,3,2048,256,3]{3,2,4,1,0:T(8,128)} %get-tuple-element.286, f32[2,3,3,256]{3,2,1,0:T(4,128)S(1)} %fusion.134, f32[2,3,3,256]{3,2,1,0:T(4,128)S(1)} %get-tuple-element.287, ...), kind=kOutput, calls=%fused_computation.7.clone.1 | convolution fusion | flops 1255440384 | bytes 40996864 | tf_op jit(solution)/shard_map/while/body/eval_jaxpr/rkgqs,rskd->rqkgd/dot_general | solution.py:129
  262.5 16.0 %fusion.133 = (f32[2,3,3,256]{3,2,1,0:T(4,128)S(1)}, f32[2,3,2048,256,3]{3,2,4,1,0:T(8,128)}) fusion(pred[2,256,2048]{1,2,0:T(8,128)(4,1)S(1)} %dynamic-slice_bitcast_fusion.6, bf16[2,2048,3,64,1]{1,3,4,2,0:T(8,128)(2,1)S(1)} %bitcast.281, bf16[4,2,256,3,3,64]{2,5,4,3,1,0:T(8,128)(2,1)} %get-tuple-element.324, s32[]{:T(128)S(6)} %copy.57), kind=kOutput, calls=%fused_computation.4.clone.1 | convolution fusion | flops 1236266496 | bytes 40978436 | tf_op jit(solution)/shard_map/while/body/eval_jaxpr/rqkgd,rskd->rkgqs/dot_general | solution.py:114
  278.5 16.3 %fusion.134 = f32[2,3,3,256]{3,2,1,0:T(4,128)S(1)} fusion(f32[2,3,2048,256,3]{3,2,4,1,0:T(8,128)} %get-tuple-element.286, f32[2,3,3,256]{3,2,1,0:T(4,128)S(1)} %get-tuple-element.287, pred[2,256,2048]{1,2,0:T(8,128)(4,1)S(1)} %dynamic-slice_bitcast_fusion.6), kind=kLoop, calls=%fused_computation.3.clone.1 | loop fusion | flops 37744128 | bytes 38834176 | tf_op jit(solution)/shard_map/while/body/eval_jaxpr/reduce_sum | solution.py:126
  294.8 17.3 %fusion.135 = bf16[2,3,64,3,256]{4,2,3,1,0:T(8,128)(2,1)S(1)} fusion(bf16[2,2048,3,64,1]{1,3,4,2,0:T(8,128)(2,1)} %bitcast.290, f32[2,3,2048,256,3]{3,2,4,1,0:T(8,128)} %get-tuple-element.286, f32[2,3,3,256]{3,2,1,0:T(4,128)S(1)} %fusion.134, f32[2,3,3,256]{3,2,1,0:T(4,128)S(1)} %get-tuple-element.287, ...), kind=kOutput, calls=%fused_computation.7.clone.1 | convolution fusion | flops 1255440384 | bytes 40996864 | tf_op jit(solution)/shard_map/while/body/eval_jaxpr/rkgqs,rskd->rqkgd/dot_general | solution.py:129
  317.9 16.0 %fusion.133 = (f32[2,3,3,256]{3,2,1,0:T(4,128)S(1)}, f32[2,3,2048,256,3]{3,2,4,1,0:T(8,128)}) fusion(pred[2,256,2048]{1,2,0:T(8,128)(4,1)S(1)} %dynamic-slice_bitcast_fusion.6, bf16[2,2048,3,64,1]{1,3,4,2,0:T(8,128)(2,1)S(1)} %bitcast.281, bf16[4,2,256,3,3,64]{2,5,4,3,1,0:T(8,128)(2,1)} %get-tuple-element.324, s32[]{:T(128)S(6)} %copy.57), kind=kOutput, calls=%fused_computation.4.clone.1 | convolution fusion | flops 1236266496 | bytes 40978436 | tf_op jit(solution)/shard_map/while/body/eval_jaxpr/rqkgd,rskd->rkgqs/dot_general | solution.py:114
  333.9 16.3 %fusion.134 = f32[2,3,3,256]{3,2,1,0:T(4,128)S(1)} fusion(f32[2,3,2048,256,3]{3,2,4,1,0:T(8,128)} %get-tuple-element.286, f32[2,3,3,256]{3,2,1,0:T(4,128)S(1)} %get-tuple-element.287, pred[2,256,2048]{1,2,0:T(8,128)(4,1)S(1)} %dynamic-slice_bitcast_fusion.6), kind=kLoop, calls=%fused_computation.3.clone.1 | loop fusion | flops 37744128 | bytes 38834176 | tf_op jit(solution)/shard_map/while/body/eval_jaxpr/reduce_sum | solution.py:126
  350.2 17.3 %fusion.135 = bf16[2,3,64,3,256]{4,2,3,1,0:T(8,128)(2,1)S(1)} fusion(bf16[2,2048,3,64,1]{1,3,4,2,0:T(8,128)(2,1)} %bitcast.290, f32[2,3,2048,256,3]{3,2,4,1,0:T(8,128)} %get-tuple-element.286, f32[2,3,3,256]{3,2,1,0:T(4,128)S(1)} %fusion.134, f32[2,3,3,256]{3,2,1,0:T(4,128)S(1)} %get-tuple-element.287, ...), kind=kOutput, calls=%fused_computation.7.clone.1 | convolution fusion | flops 1255440384 | bytes 40996864 | tf_op jit(solution)/shard_map/while/body/eval_jaxpr/rkgqs,rskd->rqkgd/dot_general | solution.py:129
  376.8 8.0 fusion.51
  384.8 8.0 fusion.55
  392.9 22.0 %multiply_convert_fusion = (bf16[8,256,1536]{2,1,0:T(8,128)(2,1)}, bf16[8,256,1536]{2,1,0:T(8,128)(2,1)}, bf16[8,256,1536]{2,1,0:T(8,128)(2,1)}) fusion(f32[8,256,1536]{2,1,0:T(8,128)} %fusion.55, f32[8,256,1536]{2,1,0:T(8,128)} %fusion.51, bf16[1536,576]{0,1:T(8,128)(2,1)S(1)} %copy-done, bf16[8,256,576]{1,2,0:T(8,128)(2,1)} %param.27, ...), kind=kOutput, calls=%fused_computation.48 | convolution fusion | flops 3674603520 | bytes 48177152 | tf_op jit(solution)/shard_map/rte,de->rtd/dot_general | solution.py:51
  431.7 481.4 %while.27 = (s32[]{:T(128)}, f32[4,2,256,576]{2,3,1,0:T(8,128)}, bf16[4,2,2048,192]{2,3,1,0:T(8,128)(2,1)}, bf16[4,2,2048,192]{2,3,1,0:T(8,128)(2,1)}, bf16[4,2,...) while((s32[]{:T(128)}, f32[4,2,256,576]{2,3,1,0:T(8,128)}, ...), condition=%wide.region_9.10_spmd, body=%wide.region_7.9_spmd.sunk | while | flops 6183218688 | bytes 328595648 | solution.py:207
  438.8 15.8 %fusion.146 = f32[2,3,2048,256,3]{3,2,4,1,0:T(8,128)} fusion(bf16[2,2048,3,64,1]{1,3,4,2,0:T(8,128)(2,1)S(1)} %bitcast.279, bf16[4,2,256,3,3,64]{2,5,4,3,1,0:T(8,128)(2,1)} %get-tuple-element.354, s32[]{:T(128)S(6)} %copy.67), kind=kOutput, calls=%fused_computation.33.clone.1 | convolution fusion | flops 1207959552 | bytes 39911428 | tf_op jit(solution)/shard_map/while/body/eval_jaxpr/rqkgd,rskd->rkgqs/dot_general | solution.py:114
  454.5 17.5 %fusion.149 = bf16[2,3,64,2048,1]{3,2,4,1,0:T(8,128)(2,1)} fusion(bf16[2,256,3,3,64]{1,4,3,2,0:T(8,128)(2,1)S(1)} %bitcast.285, f32[2,3,2048,256,3]{3,2,4,1,0:T(8,128)} %fusion.146, f32[2,3,3,256]{3,2,1,0:T(4,128)S(1)} %dynamic-slice_bitcast_fusion.7, pred[2,256,2048]{1,2,0:T(8,128)(4,1)S(1)} %dynamic-slice_bitcast_fusion.8), kind=kOutput, calls=%fused_computation.27.clone.1 | convolution fusion | flops 1245708288 | bytes 40978432 | tf_op jit(solution)/shard_map/while/body/eval_jaxpr/rkgqs,rqkgd->rskd/dot_general | solution.py:195
  472.1 25.9 %fusion.147 = (f32[2,3,3,256]{3,2,1,0:T(4,128)S(1)}, f32[2,3,2048,256,3]{3,2,4,1,0:T(8,128)}) fusion(f32[2,3,2048,256,3]{3,2,4,1,0:T(8,128)} %fusion.146, f32[2,3,3,256]{3,2,1,0:T(4,128)S(1)} %dynamic-slice_bitcast_fusion.7, pred[2,256,2048]{1,2,0:T(8,128)(4,1)S(1)} %dynamic-slice_bitcast_fusion.8, bf16[2,2048,3,64,1]{1,3,4,2,0:T(8,128)(2,1)S(1)} %bitcast.283, ...), kind=kOutput, calls=%fused_computation.20.clone.1 | convolution fusion | flops 1255140864 | bytes 78745600 | tf_op jit(solution)/shard_map/while/body/eval_jaxpr/rqkgd,rskd->rkgqs/dot_general | solution.py:178
  497.9 31.4 %fusion.148 = bf16[2,3,3,256,2048]{3,4,2,1,0:T(8,128)(2,1)} fusion(f32[2,3,2048,256,3]{3,2,4,1,0:T(8,128)} %get-tuple-element.298, f32[2,3,2048,256,3]{3,2,4,1,0:T(8,128)} %fusion.146, f32[2,3,3,256]{3,2,1,0:T(4,128)S(1)} %get-tuple-element.299, f32[2,3,3,256]{3,2,1,0:T(4,128)S(1)} %dynamic-slice_bitcast_fusion.7, ...), kind=kLoop, calls=%fused_computation.22.clone.1 | loop fusion | flops 56623104 | bytes 95457280 | tf_op jit(solution)/shard_map/while/body/eval_jaxpr/convert_element_type | solution.py:182
  529.3 9.9 convolution_multiply_fusion.2
  539.2 9.9 bitcast_multiply_fusion.5
  559.0 15.8 %fusion.146 = f32[2,3,2048,256,3]{3,2,4,1,0:T(8,128)} fusion(bf16[2,2048,3,64,1]{1,3,4,2,0:T(8,128)(2,1)S(1)} %bitcast.279, bf16[4,2,256,3,3,64]{2,5,4,3,1,0:T(8,128)(2,1)} %get-tuple-element.354, s32[]{:T(128)S(6)} %copy.67), kind=kOutput, calls=%fused_computation.33.clone.1 | convolution fusion | flops 1207959552 | bytes 39911428 | tf_op jit(solution)/shard_map/while/body/eval_jaxpr/rqkgd,rskd->rkgqs/dot_general | solution.py:114
  574.8 17.5 %fusion.149 = bf16[2,3,64,2048,1]{3,2,4,1,0:T(8,128)(2,1)} fusion(bf16[2,256,3,3,64]{1,4,3,2,0:T(8,128)(2,1)S(1)} %bitcast.285, f32[2,3,2048,256,3]{3,2,4,1,0:T(8,128)} %fusion.146, f32[2,3,3,256]{3,2,1,0:T(4,128)S(1)} %dynamic-slice_bitcast_fusion.7, pred[2,256,2048]{1,2,0:T(8,128)(4,1)S(1)} %dynamic-slice_bitcast_fusion.8), kind=kOutput, calls=%fused_computation.27.clone.1 | convolution fusion | flops 1245708288 | bytes 40978432 | tf_op jit(solution)/shard_map/while/body/eval_jaxpr/rkgqs,rqkgd->rskd/dot_general | solution.py:195
  592.3 25.9 %fusion.147 = (f32[2,3,3,256]{3,2,1,0:T(4,128)S(1)}, f32[2,3,2048,256,3]{3,2,4,1,0:T(8,128)}) fusion(f32[2,3,2048,256,3]{3,2,4,1,0:T(8,128)} %fusion.146, f32[2,3,3,256]{3,2,1,0:T(4,128)S(1)} %dynamic-slice_bitcast_fusion.7, pred[2,256,2048]{1,2,0:T(8,128)(4,1)S(1)} %dynamic-slice_bitcast_fusion.8, bf16[2,2048,3,64,1]{1,3,4,2,0:T(8,128)(2,1)S(1)} %bitcast.283, ...), kind=kOutput, calls=%fused_computation.20.clone.1 | convolution fusion | flops 1255140864 | bytes 78745600 | tf_op jit(solution)/shard_map/while/body/eval_jaxpr/rqkgd,rskd->rkgqs/dot_general | solution.py:178
  618.2 31.4 %fusion.148 = bf16[2,3,3,256,2048]{3,4,2,1,0:T(8,128)(2,1)} fusion(f32[2,3,2048,256,3]{3,2,4,1,0:T(8,128)} %get-tuple-element.298, f32[2,3,2048,256,3]{3,2,4,1,0:T(8,128)} %fusion.146, f32[2,3,3,256]{3,2,1,0:T(4,128)S(1)} %get-tuple-element.299, f32[2,3,3,256]{3,2,1,0:T(4,128)S(1)} %dynamic-slice_bitcast_fusion.7, ...), kind=kLoop, calls=%fused_computation.22.clone.1 | loop fusion | flops 56623104 | bytes 95457280 | tf_op jit(solution)/shard_map/while/body/eval_jaxpr/convert_element_type | solution.py:182
  649.5 9.9 convolution_multiply_fusion.2
  659.4 9.9 bitcast_multiply_fusion.5
  679.3 15.8 %fusion.146 = f32[2,3,2048,256,3]{3,2,4,1,0:T(8,128)} fusion(bf16[2,2048,3,64,1]{1,3,4,2,0:T(8,128)(2,1)S(1)} %bitcast.279, bf16[4,2,256,3,3,64]{2,5,4,3,1,0:T(8,128)(2,1)} %get-tuple-element.354, s32[]{:T(128)S(6)} %copy.67), kind=kOutput, calls=%fused_computation.33.clone.1 | convolution fusion | flops 1207959552 | bytes 39911428 | tf_op jit(solution)/shard_map/while/body/eval_jaxpr/rqkgd,rskd->rkgqs/dot_general | solution.py:114
  695.0 17.5 %fusion.149 = bf16[2,3,64,2048,1]{3,2,4,1,0:T(8,128)(2,1)} fusion(bf16[2,256,3,3,64]{1,4,3,2,0:T(8,128)(2,1)S(1)} %bitcast.285, f32[2,3,2048,256,3]{3,2,4,1,0:T(8,128)} %fusion.146, f32[2,3,3,256]{3,2,1,0:T(4,128)S(1)} %dynamic-slice_bitcast_fusion.7, pred[2,256,2048]{1,2,0:T(8,128)(4,1)S(1)} %dynamic-slice_bitcast_fusion.8), kind=kOutput, calls=%fused_computation.27.clone.1 | convolution fusion | flops 1245708288 | bytes 40978432 | tf_op jit(solution)/shard_map/while/body/eval_jaxpr/rkgqs,rqkgd->rskd/dot_general | solution.py:195
  712.6 25.9 %fusion.147 = (f32[2,3,3,256]{3,2,1,0:T(4,128)S(1)}, f32[2,3,2048,256,3]{3,2,4,1,0:T(8,128)}) fusion(f32[2,3,2048,256,3]{3,2,4,1,0:T(8,128)} %fusion.146, f32[2,3,3,256]{3,2,1,0:T(4,128)S(1)} %dynamic-slice_bitcast_fusion.7, pred[2,256,2048]{1,2,0:T(8,128)(4,1)S(1)} %dynamic-slice_bitcast_fusion.8, bf16[2,2048,3,64,1]{1,3,4,2,0:T(8,128)(2,1)S(1)} %bitcast.283, ...), kind=kOutput, calls=%fused_computation.20.clone.1 | convolution fusion | flops 1255140864 | bytes 78745600 | tf_op jit(solution)/shard_map/while/body/eval_jaxpr/rqkgd,rskd->rkgqs/dot_general | solution.py:178
  738.4 31.4 %fusion.148 = bf16[2,3,3,256,2048]{3,4,2,1,0:T(8,128)(2,1)} fusion(f32[2,3,2048,256,3]{3,2,4,1,0:T(8,128)} %get-tuple-element.298, f32[2,3,2048,256,3]{3,2,4,1,0:T(8,128)} %fusion.146, f32[2,3,3,256]{3,2,1,0:T(4,128)S(1)} %get-tuple-element.299, f32[2,3,3,256]{3,2,1,0:T(4,128)S(1)} %dynamic-slice_bitcast_fusion.7, ...), kind=kLoop, calls=%fused_computation.22.clone.1 | loop fusion | flops 56623104 | bytes 95457280 | tf_op jit(solution)/shard_map/while/body/eval_jaxpr/convert_element_type | solution.py:182
  769.8 9.9 convolution_multiply_fusion.2
  779.7 9.9 bitcast_multiply_fusion.5
  799.5 15.8 %fusion.146 = f32[2,3,2048,256,3]{3,2,4,1,0:T(8,128)} fusion(bf16[2,2048,3,64,1]{1,3,4,2,0:T(8,128)(2,1)S(1)} %bitcast.279, bf16[4,2,256,3,3,64]{2,5,4,3,1,0:T(8,128)(2,1)} %get-tuple-element.354, s32[]{:T(128)S(6)} %copy.67), kind=kOutput, calls=%fused_computation.33.clone.1 | convolution fusion | flops 1207959552 | bytes 39911428 | tf_op jit(solution)/shard_map/while/body/eval_jaxpr/rqkgd,rskd->rkgqs/dot_general | solution.py:114
  815.3 17.5 %fusion.149 = bf16[2,3,64,2048,1]{3,2,4,1,0:T(8,128)(2,1)} fusion(bf16[2,256,3,3,64]{1,4,3,2,0:T(8,128)(2,1)S(1)} %bitcast.285, f32[2,3,2048,256,3]{3,2,4,1,0:T(8,128)} %fusion.146, f32[2,3,3,256]{3,2,1,0:T(4,128)S(1)} %dynamic-slice_bitcast_fusion.7, pred[2,256,2048]{1,2,0:T(8,128)(4,1)S(1)} %dynamic-slice_bitcast_fusion.8), kind=kOutput, calls=%fused_computation.27.clone.1 | convolution fusion | flops 1245708288 | bytes 40978432 | tf_op jit(solution)/shard_map/while/body/eval_jaxpr/rkgqs,rqkgd->rskd/dot_general | solution.py:195
  832.8 25.9 %fusion.147 = (f32[2,3,3,256]{3,2,1,0:T(4,128)S(1)}, f32[2,3,2048,256,3]{3,2,4,1,0:T(8,128)}) fusion(f32[2,3,2048,256,3]{3,2,4,1,0:T(8,128)} %fusion.146, f32[2,3,3,256]{3,2,1,0:T(4,128)S(1)} %dynamic-slice_bitcast_fusion.7, pred[2,256,2048]{1,2,0:T(8,128)(4,1)S(1)} %dynamic-slice_bitcast_fusion.8, bf16[2,2048,3,64,1]{1,3,4,2,0:T(8,128)(2,1)S(1)} %bitcast.283, ...), kind=kOutput, calls=%fused_computation.20.clone.1 | convolution fusion | flops 1255140864 | bytes 78745600 | tf_op jit(solution)/shard_map/while/body/eval_jaxpr/rqkgd,rskd->rkgqs/dot_general | solution.py:178
  858.6 31.4 %fusion.148 = bf16[2,3,3,256,2048]{3,4,2,1,0:T(8,128)(2,1)} fusion(f32[2,3,2048,256,3]{3,2,4,1,0:T(8,128)} %get-tuple-element.298, f32[2,3,2048,256,3]{3,2,4,1,0:T(8,128)} %fusion.146, f32[2,3,3,256]{3,2,1,0:T(4,128)S(1)} %get-tuple-element.299, f32[2,3,3,256]{3,2,1,0:T(4,128)S(1)} %dynamic-slice_bitcast_fusion.7, ...), kind=kLoop, calls=%fused_computation.22.clone.1 | loop fusion | flops 56623104 | bytes 95457280 | tf_op jit(solution)/shard_map/while/body/eval_jaxpr/convert_element_type | solution.py:182
  890.0 9.9 convolution_multiply_fusion.2
  899.9 9.9 bitcast_multiply_fusion.5
  944.5 36.7 %reduce-scatter.3.cloned.1.call-done = bf16[8,256,192]{1,2,0:T(8,128)(2,1)} async-done(((bf16[8,2048,192]{1,2,0:T(8,128)(2,1)}), bf16[8,256,192]{1,2,0:T(8,128)(2,1)}) %reduce-scatter.3.cloned.1.call-update) | async-done | bytes 786448 | tf_op jit(solution)/shard_map/reduce_scatter | solution.py:221
  986.2 65.4 %reduce-scatter.5.cloned.1.call-done = bf16[8,256,192]{1,2,0:T(8,128)(2,1)} async-done(((bf16[8,2048,192]{1,2,0:T(8,128)(2,1)}), bf16[8,256,192]{1,2,0:T(8,128)(2,1)}) %reduce-scatter.5.cloned.1.call-update) | async-done | bytes 786448 | tf_op jit(solution)/shard_map/reduce_scatter | solution.py:224
  1060.4 9.5 multiply_convert_fusion.3
  1075.8 38.9 %all-reduce = (f32[576]{0:T(1024)}, f32[576]{0:T(1024)}) all-reduce(f32[576]{0:T(1024)S(1)} %get-tuple-element.110, f32[576]{0:T(1024)S(1)} %copy-done.35), channel_id=1, replica_groups=mesh['batch'=4,'seq'=8] {'batch','seq'}, use_global_device_ids=true, to_apply=%region_14.15 | all-reduce | flops 1152 | bytes 9216 | tf_op jit(solution)/shard_map/psum | solution.py:259
  1122.0 196.1 %all-reduce.4.cloned.1.call-done = (f32[576,576]{1,0:T(8,128)}, f32[576,192]{0,1:T(8,128)}, f32[576,192]{0,1:T(8,128)}, f32[576,576]{1,0:T(8,128)}, f32[576,1536...) async-done(((f32[576,576]{1,0:T(8,128)}, f32[576,192]{0,1:T(8,128)}, f32[576,192]{0,1:T(8,128)}, f32[576,576]{1,0:T(8,128)}, f32[576,1536]{1,0:T(8,128)}, ...) | async-done | bytes 14155792 | tf_op jit(solution)/shard_map/psum | solution.py:259
  (243 shorter events, 186.3 us)
Async XLA Ops:
  7.2 385.7 %copy-start = (bf16[1536,576]{0,1:T(8,128)(2,1)S(1)}, bf16[1536,576]{0,1:T(8,128)(2,1)}, u32[]{:S(2)}) copy-start(bf16[1536,576]{0,1:T(8,128)(2,1)} %param.26) | copy-start | bytes 5308420
  7.2 6.1 copy-start.33
  7.2 6.1 copy-start.25
  7.2 73.8 %all-gather.3.cloned.1.call-start = ((), (), s32[]{:S(2)}) async-start(), calls=%async_computation.2 | async-start | bytes 7077888 | tf_op jit(solution)/shard_map/all_gather | solution.py:108
  9.5 9.4 copy-start.28
  13.0 133.6 %all-gather.5.cloned.1.call-start = ((), (), s32[]{:S(2)}) async-start(), calls=%async_computation.3 | async-start | bytes 7077888 | tf_op jit(solution)/shard_map/all_gather | solution.py:107
  13.3 10.4 copy-start.20
  13.3 10.4 copy-start.22
  16.0 2.1 copy-start.36
  16.1 2.9 copy-start.42
  18.1 963.2 %reduce-scatter.3.cloned.1.call-start = ((), (), s32[]{:S(2)}) async-start(), calls=%async_computation.4 | async-start | bytes 7077888 | tf_op jit(solution)/shard_map/reduce_scatter | solution.py:221
  368.9 5.1 copy-start.32
  374.0 10.8 copy-start.7
  374.0 2.8 copy-start.39
  376.8 8.0 copy-start.15
  376.8 8.0 copy-start.38
  384.8 8.0 copy-start.30
  414.8 6.7 copy-start.8
  414.8 6.7 copy-start.40
  414.8 7.1 copy-start.44
  421.9 5.0 copy-start.13
  428.3 3.4 copy-start.6
  539.2 11.0 copy-start.2
  659.4 11.0 copy-start.2
  779.7 11.0 copy-start.2
  899.9 11.0 copy-start.2
  913.1 138.5 %reduce-scatter.5.cloned.1.call-start = ((), (), s32[]{:S(2)}) async-start(), calls=%async_computation.5 | async-start | bytes 7077888 | tf_op jit(solution)/shard_map/reduce_scatter | solution.py:224
  913.7 404.5 %all-reduce.4.cloned.1.call-start = ((), (), s32[]{:S(2)}) async-start(), calls=%async_computation.6 | async-start | bytes 29097984 | tf_op jit(solution)/shard_map/psum | solution.py:259
  916.7 2.6 slice-start.2
  919.5 4.9 slice-start
  921.2 3.2 copy-start.17
  921.2 3.2 slice-start.1
  921.2 3.2 copy-start.37
  921.2 6.4 slice-start.4
  924.4 3.2 copy-start.16
  924.4 3.2 slice-start.5
  924.4 8.8 slice-start.8
  927.6 5.6 slice-start.9
  927.6 11.3 slice-start.6
  933.2 5.6 copy-start.14
  933.2 5.6 copy-start.31
  933.2 5.6 slice-start.7
  944.5 38.4 %copy-start.19 = (f32[256,3,64]{0,2,1:T(8,128)S(1)}, f32[256,3,64]{0,2,1:T(8,128)}, u32[]{:S(2)}) copy-start(f32[256,3,64]{0,2,1:T(8,128)} %copy-done.18) | copy-start | bytes 589828
  1060.4 9.5 copy-start.26
  1071.9 3.9 copy-start.35
  1318.2 9.1 copy-start.11
  1324.6 4.5 copy-start.10
  1329.1 3.3 copy-start.9
  (18 other events, 26.1 us)
Sparse Core Ops, SparseCore 0:
  13.1 67.8 all-gather.2
  83.2 63.3 all-gather.4
  913.2 67.9 reduce-scatter.2
  983.4 68.1 reduce-scatter.4
  1059.0 259.1 all-reduce.3
where the time goes:
time: 1350 us; the launch traced here: 1340 us
  matrix products  564 us (42%)
  waiting for transfers between devices  413 us (31%)
  other arithmetic  221 us (16%)
  local copies, waits for them, and re-layouts  87.8 us (7%)
  blocking collectives  38.9 us (3%)
  between operations  14.9 us (1%)
    psum x1, waiting for transfers between devices, body(): lax.psum((grad_gain_attn, grad_query_w, grad_key_w, grad_value_w, grad_ou...  196 us
    dot_general x8, matrix products, scores_of(): jnp.einsum('rqkgd,rskd->rkgqs', query_block, key_heads, preferred_element...  127 us
    convert_element_type x4, other arithmetic, backward_block(): grad_scores = (probs * (grad_probs - row_inner)).astype(jnp.bfloat16)  126 us
    dot_general x4, matrix products, backward_block(): jnp.einsum('rqkgd,rskd->rkgqs', grad_heads, value_heads, preferred_elemen...  103 us
    dot_general x4, matrix products, backward_block(): jnp.einsum('rkgqs,rqkgd->rskd', probs.astype(jnp.bfloat16), grad_heads, p...  70.1 us
    dot_general x4, matrix products, forward_block(): jnp.einsum('rkgqs,rskd->rqkgd', probs, value_heads, preferred_element_typ...  69.3 us
    all_gather x1, waiting for transfers between devices, body(): lax.all_gather(key_rows, 'seq', axis=1, tiled=True)  65.6 us
    reduce_scatter x1, waiting for transfers between devices, body(): lax.psum_scatter(grad_value.astype(jnp.bfloat16), 'seq', scatter_dimensio...  65.4 us
  transfers between devices with their start and end apart: 5, of which 5 were waited for; matrix products, arithmetic and copies ran while one was open for 6% of the time, Pallas kernels for 0%

commit v1 on v0

v1 whole, which is shorter than its diff:
```python
import functools

import jax
import jax.numpy as jnp
from jax import lax
from jax.experimental import pallas as pl
from jax.experimental.pallas import tpu as pltpu
from jax.sharding import PartitionSpec as P

H = 9
KVH = 3
HD = 64
GROUP = H // KVH

EPSILON = 1e-05
ROPE_BASE = 10000.0
MASKED_SCORE = -1e30
BF16 = jnp.bfloat16
F32 = jnp.float32
VMEM_LIMIT = 56 * 1024 * 1024


def dot(a, b, a_dim, b_dim):
    return lax.dot_general(a, b, (((a_dim,), (b_dim,)), ((), ())), preferred_element_type=F32)


def rope_tables(positions):
    freqs = ROPE_BASE ** (-(jnp.arange(HD // 2, dtype=F32) * 2.0) / HD)
    phases = freqs[:, None] * positions[None, :]
    return jnp.cos(phases), jnp.sin(phases)


def rms_scale(vectors):
    return lax.rsqrt(jnp.mean(vectors * vectors, axis=-1, keepdims=True) + EPSILON)


def norm_back(grad_normed, normed, inv_scale):
    return inv_scale * (
        grad_normed - normed * jnp.mean(grad_normed * normed, axis=-1, keepdims=True)
    )


def project(vectors, matrix):
    return jnp.einsum("rtd,de->rte", vectors, matrix, preferred_element_type=F32)


def project_back(gradient, matrix):
    return jnp.einsum("rte,de->rtd", gradient, matrix, preferred_element_type=F32)


def weight_grad(vectors, gradient):
    return jnp.einsum("rtd,rte->de", vectors, gradient, preferred_element_type=F32)


def qkv_kernel(info, x_ref, gain_ref, w_ref, cos_ref, sin_ref, q_ref, kv_ref, n_ref):
    used = info[0] < info[3 + pl.program_id(0)]

    @pl.when(used)
    def _():
        x = x_ref[0].astype(F32)
        normed = (x * rms_scale(x) * gain_ref[...]).astype(BF16)
        n_ref[0] = normed
        out = dot(w_ref[...], normed, 1, 1)
        cos, sin = cos_ref[...], sin_ref[...]

        def rope(block):
            u1, u2 = block[: HD // 2], block[HD // 2 :]
            return jnp.concatenate([u1 * cos - u2 * sin, u2 * cos + u1 * sin], axis=0)

        for h in range(H):
            rotated = rope(out[h * HD : (h + 1) * HD])
            q_ref[0, h * HD : (h + 1) * HD, :] = (rotated * HD**-0.5).astype(BF16)
        for k in range(KVH):
            base = H * HD + 2 * HD * k
            kv_ref[0, 2 * HD * k : 2 * HD * k + HD, :] = rope(out[base : base + HD]).astype(BF16)
            kv_ref[0, 2 * HD * k + HD : 2 * HD * (k + 1), :] = out[base + HD : base + 2 * HD].astype(
                BF16
            )

    @pl.when(jnp.logical_not(used))
    def _():
        q_ref[...] = jnp.zeros_like(q_ref)
        kv_ref[...] = jnp.zeros_like(kv_ref)
        n_ref[...] = jnp.zeros_like(n_ref)


def row_spec(shape):
    return pl.BlockSpec((1,) + shape, lambda r, info: (r, 0, 0))


def whole_spec(shape):
    return pl.BlockSpec(shape, lambda r, info: (0,) * len(shape))


def qkv_call(info, tokens, gain, weights, cos, sin):
    rows, length, width = tokens.shape
    return pl.pallas_call(
        qkv_kernel,
        grid_spec=pltpu.PrefetchScalarGridSpec(
            num_scalar_prefetch=1,
            grid=(rows,),
            in_specs=[
                row_spec((length, width)),
                whole_spec((1, width)),
                whole_spec(weights.shape),
                whole_spec(cos.shape),
                whole_spec(sin.shape),
            ],
            out_specs=[
                row_spec((H * HD, length)),
                row_spec((2 * KVH * HD, length)),
                row_spec((length, width)),
            ],
        ),
        out_shape=[
            jax.ShapeDtypeStruct((rows, H * HD, length), BF16),
            jax.ShapeDtypeStruct((rows, 2 * KVH * HD, length), BF16),
            jax.ShapeDtypeStruct((rows, length, width), BF16),
        ],
        compiler_params=pltpu.CompilerParams(vmem_limit_bytes=VMEM_LIMIT),
        name="qkv",
    )(info, tokens, gain, weights, cos, sin)


def heads_of(ref, k):
    return jnp.concatenate(
        [ref[0, (k * GROUP + g) * HD : (k * GROUP + g + 1) * HD, :] for g in range(GROUP)], axis=1
    )


def key_value(ref, k):
    return ref[0, 2 * HD * k : 2 * HD * k + HD, :], ref[0, 2 * HD * k + HD : 2 * HD * (k + 1), :]


def mask_diagonal(scores, start, length):
    size = scores.shape[0]
    key = lax.broadcasted_iota(jnp.int32, scores.shape, 0)
    query = lax.broadcasted_iota(jnp.int32, scores.shape, 1) % size
    allowed = jnp.logical_and(key <= query, start + key < length)
    return jnp.where(allowed, scores, MASKED_SCORE)


def visit_blocks(info, chips, kv_refs, visit):
    chip, core = info[1], info[2]

    @pl.when(core == 0)
    def _():
        visit([(0, True)], True)

    @pl.when(core == 1)
    def _():
        visit([(0, True), (1, False)], True)

    for d in range(1, chips):

        @pl.when(chip >= d)
        def _():
            visit([(2 * d, False), (2 * d + 1, False)], False)


def forward_kernel(chips, info, q_ref, *refs):
    kv_refs = refs[: 2 * chips]
    mixed_ref, lse_ref, peak_ref, total_ref, acc_ref = refs[2 * chips :]
    start, length = info[0], info[3 + pl.program_id(0)]
    used = start < length

    def visit(blocks, first):
        for k in range(KVH):
            queries = heads_of(q_ref, k)
            scores = []
            for b, diagonal in blocks:
                s = dot(key_value(kv_refs[b], k)[0], queries, 0, 0)
                scores.append(mask_diagonal(s, start, length) if diagonal else s)
            peak = scores[0].max(axis=0, keepdims=True)
            for s in scores[1:]:
                peak = jnp.maximum(peak, s.max(axis=0, keepdims=True))
            if not first:
                old = peak_ref[k]
                peak = jnp.maximum(peak, old)
                shrink = jnp.exp(old - peak)
            total, acc = 0.0, 0.0
            for (b, _), s in zip(blocks, scores):
                weights = jnp.exp(s - peak)
                total = total + weights.sum(axis=0, keepdims=True)
                acc = acc + dot(key_value(kv_refs[b], k)[1], weights.astype(BF16), 1, 0)
            if not first:
                total = total + total_ref[k] * shrink
                acc = acc + acc_ref[k] * shrink
            peak_ref[k], total_ref[k], acc_ref[k] = peak, total, acc

    @pl.when(used)
    def _():
        visit_blocks(info, chips, kv_refs, visit)
        size = q_ref.shape[2]
        parts = []
        for k in range(KVH):
            total = total_ref[k]
            out = acc_ref[k] / total
            lse = peak_ref[k] + jnp.log(total)
            for g in range(GROUP):
                lse_ref[0, k * GROUP + g : k * GROUP + g + 1, :] = lse[:, g * size : (g + 1) * size]
                parts.append(out[:, g * size : (g + 1) * size])
        mixed_ref[0] = jnp.concatenate(parts, axis=0).T.astype(BF16)

    @pl.when(jnp.logical_not(used))
    def _():
        mixed_ref[...] = jnp.zeros_like(mixed_ref)
        lse_ref[...] = jnp.zeros_like(lse_ref)


def forward_call(info, queries, kv_blocks):
    rows, _, length = queries.shape
    blocks = len(kv_blocks)
    return pl.pallas_call(
        functools.partial(forward_kernel, blocks // 2),
        grid_spec=pltpu.PrefetchScalarGridSpec(
            num_scalar_prefetch=1,
            grid=(rows,),
            in_specs=[row_spec((H * HD, length))] + [row_spec((2 * KVH * HD, length))] * blocks,
            out_specs=[row_spec((length, H * HD)), row_spec((H, length))],
            scratch_shapes=[
                pltpu.VMEM((KVH, 1, GROUP * length), F32),
                pltpu.VMEM((KVH, 1, GROUP * length), F32),
                pltpu.VMEM((KVH, HD, GROUP * length), F32),
            ],
        ),
        out_shape=[
            jax.ShapeDtypeStruct((rows, length, H * HD), BF16),
            jax.ShapeDtypeStruct((rows, H, length), F32),
        ],
        compiler_params=pltpu.CompilerParams(vmem_limit_bytes=VMEM_LIMIT),
        name="attention_forward",
    )(info, queries, *kv_blocks)


def backward_kernel(chips, info, q_ref, dmix_ref, mixed_ref, lse_ref, cos_ref, sin_ref, *refs):
    kv_refs = refs[: 2 * chips]
    dq_ref = refs[2 * chips]
    dkv_refs = refs[2 * chips + 1 : 4 * chips + 1]
    dmix_t_ref, inner_ref, dq_acc_ref = refs[4 * chips + 1 :]
    start, length = info[0], info[3 + pl.program_id(0)]
    chip, core = info[1], info[2]
    used = start < length
    size = q_ref.shape[2]

    def visit(blocks, first):
        for k in range(KVH):
            queries, dmix = heads_of(q_ref, k), heads_of(dmix_t_ref, k)
            lse = jnp.concatenate(
                [lse_ref[0, k * GROUP + g : k * GROUP + g + 1, :] for g in range(GROUP)], axis=1
            )
            inner = inner_ref[k]
            dq = None
            for b, diagonal in blocks:
                keys, values = key_value(kv_refs[b], k)
                s = dot(keys, queries, 0, 0)
                if diagonal:
                    s = mask_diagonal(s, start, length)
                probs = jnp.exp(s - lse)
                dprobs = dot(values, dmix, 0, 0)
                dscores = (probs * (dprobs - inner)).astype(BF16)
                part = dot(keys, dscores, 1, 0)
                dq = part if dq is None else dq + part
                dk = dot(dscores, queries, 1, 1)
                dv = dot(probs.astype(BF16), dmix, 1, 1)
                dkv_refs[b][0, :, 2 * HD * k : 2 * HD * (k + 1)] = jnp.concatenate(
                    [dk, dv], axis=1
                ).astype(BF16)
            if first:
                dq_acc_ref[k] = dq
            else:
                dq_acc_ref[k] += dq

    def clear(ref):
        ref[...] = jnp.zeros_like(ref)

    @pl.when(used)
    def _():
        dmix_t = dmix_ref[0].astype(F32).T
        mixed_t = mixed_ref[0].astype(F32).T
        dmix_t_ref[0] = dmix_t.astype(BF16)
        product = dmix_t * mixed_t
        for k in range(KVH):
            inner_ref[k] = jnp.concatenate(
                [
                    product[(k * GROUP + g) * HD : (k * GROUP + g + 1) * HD].sum(axis=0, keepdims=True)
                    for g in range(GROUP)
                ],
                axis=1,
            )
        visit_blocks(info, chips, kv_refs, visit)
        cos, sin = cos_ref[...], sin_ref[...]
        parts = []
        for k in range(KVH):
            dq = dq_acc_ref[k] * HD**-0.5
            for g in range(GROUP):
                head = dq[:, g * size : (g + 1) * size]
                u1, u2 = head[: HD // 2], head[HD // 2 :]
                parts += [u1 * cos + u2 * sin, u2 * cos - u1 * sin]
        dq_ref[0] = jnp.concatenate(parts, axis=0).T.astype(BF16)

    @pl.when(jnp.logical_not(used))
    def _():
        clear(dq_ref)
        clear(dkv_refs[0])

    @pl.when(jnp.logical_or(jnp.logical_not(used), core == 0))
    def _():
        clear(dkv_refs[1])

    for d in range(1, chips):

        @pl.when(jnp.logical_or(jnp.logical_not(used), chip < d))
        def _():
            clear(dkv_refs[2 * d])
            clear(dkv_refs[2 * d + 1])


def backward_call(info, queries, dmix, mixed, lse, cos, sin, kv_blocks):
    rows, _, length = queries.shape
    blocks = len(kv_blocks)
    return pl.pallas_call(
        functools.partial(backward_kernel, blocks // 2),
        grid_spec=pltpu.PrefetchScalarGridSpec(
            num_scalar_prefetch=1,
            grid=(rows,),
            in_specs=[
                row_spec((H * HD, length)),
                row_spec((length, H * HD)),
                row_spec((length, H * HD)),
                row_spec((H, length)),
                whole_spec(cos.shape),
                whole_spec(sin.shape),
            ]
            + [row_spec((2 * KVH * HD, length))] * blocks,
            out_specs=[row_spec((length, H * HD))] + [row_spec((length, 2 * KVH * HD))] * blocks,
            scratch_shapes=[
                pltpu.VMEM((1, H * HD, length), BF16),
                pltpu.VMEM((KVH, 1, GROUP * length), F32),
                pltpu.VMEM((KVH, HD, GROUP * length), F32),
            ],
        ),
        out_shape=[jax.ShapeDtypeStruct((rows, length, H * HD), BF16)]
        + [jax.ShapeDtypeStruct((rows, length, 2 * KVH * HD), BF16)] * blocks,
        compiler_params=pltpu.CompilerParams(vmem_limit_bytes=VMEM_LIMIT),
        name="attention_backward",
    )(info, queries, dmix, mixed, lse, cos, sin, *kv_blocks)


def interleave(keys, values):
    shape = keys.shape[:-1]
    pair = jnp.stack([keys.reshape(shape + (KVH, HD)), values.reshape(shape + (KVH, HD))], axis=-2)
    return pair.reshape(shape + (2 * KVH * HD,))


def separate(pairs):
    shape = pairs.shape[:-1]
    split = pairs.reshape(shape + (KVH, 2, HD))
    return (
        split[..., 0, :].reshape(shape + (KVH * HD,)),
        split[..., 1, :].reshape(shape + (KVH * HD,)),
    )


def body(
    tokens,
    lengths,
    gain_attn,
    w_query,
    w_key,
    w_value,
    w_out,
    gain_mlp,
    w_gate,
    w_up,
    w_down,
    cotangent,
):
    rows, local_len, width = tokens.shape
    seq = lax.axis_size("seq")
    chips = seq // 2
    place = lax.axis_index("seq")
    start = place * local_len
    swap = [(i, i ^ 1) for i in range(seq)]
    onward = [(i, i + 2) for i in range(seq - 2)]
    backward = [(i + 2, i) for i in range(seq - 2)]
    positions = start + jnp.arange(local_len, dtype=jnp.int32)
    cos, sin = rope_tables(positions.astype(F32))
    valid = (positions[None, :] < lengths[:, None]).astype(F32)[..., None]
    info = jnp.concatenate(
        [jnp.stack([start, place // 2, place % 2]).astype(jnp.int32), lengths]
    )
    w_kv = interleave(w_key, w_value)
    w_qkv_t = jnp.concatenate([w_query, w_kv], axis=1).T

    queries, kv_own, attn_in = qkv_call(info, tokens, gain_attn[None, :], w_qkv_t, cos, sin)
    kv_blocks = []
    moving = kv_own
    for d in range(chips):
        if d:
            moving = lax.ppermute(moving, "seq", onward)
        kv_blocks += [moving, lax.ppermute(moving, "seq", swap)]
    mixed, lse = forward_call(info, queries, kv_blocks)

    inputs = tokens.astype(F32)
    resid = inputs + project(mixed, w_out)
    mlp_scale = rms_scale(resid)
    normed_mlp = resid * mlp_scale
    mlp_in = (normed_mlp * gain_mlp).astype(BF16)
    gate_proj = project(mlp_in, w_gate)
    up_proj = project(mlp_in, w_up)
    sigmoid_gate = jax.nn.sigmoid(gate_proj)
    activated = gate_proj * sigmoid_gate
    hidden = (activated * up_proj).astype(BF16)
    layer_out = ((resid + project(hidden, w_down)) * valid).astype(BF16)
    grad_out = cotangent.astype(F32) * valid
    grad_out_low = grad_out.astype(BF16)
    grad_down = weight_grad(grad_out_low, hidden)
    grad_hidden = project_back(grad_out_low, w_down)
    grad_gate_pre = (
        grad_hidden * up_proj * sigmoid_gate * (1.0 + gate_proj * (1.0 - sigmoid_gate))
    ).astype(BF16)
    grad_up_pre = (grad_hidden * activated).astype(BF16)
    grad_gate = weight_grad(mlp_in, grad_gate_pre)
    grad_up = weight_grad(mlp_in, grad_up_pre)
    grad_mlp_in = project_back(grad_gate_pre, w_gate) + project_back(grad_up_pre, w_up)
    grad_gain_mlp = jnp.sum(grad_mlp_in * normed_mlp, axis=(0, 1))
    grad_resid = grad_out + norm_back(grad_mlp_in * gain_mlp, normed_mlp, mlp_scale)
    grad_attn = grad_resid.astype(BF16)
    grad_out_proj = weight_grad(mixed, grad_attn)
    grad_mixed = project_back(grad_attn, w_out).astype(BF16)

    grad_query_pre, *dkv_blocks = backward_call(
        info, queries, grad_mixed, mixed, lse, cos, sin, kv_blocks
    )
    total = None
    for d in reversed(range(chips)):
        own = dkv_blocks[2 * d].astype(F32) + lax.ppermute(
            dkv_blocks[2 * d + 1], "seq", swap
        ).astype(F32)
        if total is not None:
            own = own + lax.ppermute(total, "seq", backward).astype(F32)
        total = own.astype(BF16)
    grad_key, grad_value_pre = separate(total)
    keys = grad_key.astype(F32).reshape(rows, local_len, KVH, HD)
    k1, k2 = keys[..., : HD // 2], keys[..., HD // 2 :]
    cos_n, sin_n = cos.T[:, None, :], sin.T[:, None, :]
    grad_key_pre = (
        jnp.concatenate([k1 * cos_n + k2 * sin_n, k2 * cos_n - k1 * sin_n], axis=-1)
        .astype(BF16)
        .reshape(rows, local_len, KVH * HD)
    )
    attn_scale = rms_scale(inputs)
    normed_attn = inputs * attn_scale
    grad_query_w = weight_grad(attn_in, grad_query_pre)
    grad_key_w = weight_grad(attn_in, grad_key_pre)
    grad_value_w = weight_grad(attn_in, grad_value_pre)
    grad_attn_in = (
        project_back(grad_query_pre, w_query)
        + project_back(grad_key_pre, w_key)
        + project_back(grad_value_pre, w_value)
    )
    grad_gain_attn = jnp.sum(grad_attn_in * normed_attn, axis=(0, 1))
    grad_tokens = (
        grad_resid + norm_back(grad_attn_in * gain_attn, normed_attn, attn_scale)
    ).astype(BF16)

    both = ("batch", "seq")
    mlp_grads = lax.psum(
        jnp.concatenate([grad_gate, grad_up, grad_down], axis=1).astype(BF16), both
    ).astype(F32)
    attn_grads = lax.psum(
        jnp.concatenate([grad_query_w, grad_key_w, grad_value_w, grad_out_proj], axis=1).astype(
            BF16
        ),
        both,
    ).astype(F32)
    gains = lax.psum(jnp.stack([grad_gain_attn, grad_gain_mlp]), both)
    hidden_width = w_gate.shape[1]
    q_end, k_end, v_end = H * HD, (H + KVH) * HD, (H + 2 * KVH) * HD
    return (
        layer_out,
        grad_tokens,
        gains[0],
        attn_grads[:, :q_end],
        attn_grads[:, q_end:k_end],
        attn_grads[:, k_end:v_end],
        attn_grads[:, v_end:],
        gains[1],
        mlp_grads[:, :hidden_width],
        mlp_grads[:, hidden_width : 2 * hidden_width],
        mlp_grads[:, 2 * hidden_width :].T,
    )


def solution(mesh):
    split, copied = P("batch", "seq", None), P()
    in_specs = (split, P("batch")) + (copied,) * 9 + (split,)
    out_specs = (split, split) + (copied,) * 9
    return jax.shard_map(body, mesh=mesh, in_specs=in_specs, out_specs=out_specs, check_vma=False)
```

time: 1350 us -> 647 us (0.48)
  matrix products: 564 us -> 97.5 us
  other arithmetic: 221 us -> 26 us
  waiting for transfers between devices: 413 us -> 334 us
  Pallas kernels: 0 us -> 51.2 us
  local copies, waits for them, and re-layouts: 87.8 us -> 38.2 us
  starting transfers between devices: 0.2 us -> 38.6 us
    dot_general x49 -> x18, matrix products: 564 us -> 97.5 us  [the longest x7 43 us: project_back(): jnp.einsum('rte,de->rtd', gradient, matrix, preferred_element_type=F32)]
    ppermute x0 -> x14, waiting for transfers between devices: none -> 235 us  [the longest x3 132 us: body(): own = own + lax.ppermute(total, 'seq', backward).astype(F32)]
    convert_element_type x10 -> x8, other arithmetic: 132 us -> 10.4 us  [the longest x1 4.06 us: body(): mlp_grads = lax.psum(jnp.concatenate([grad_gate, grad_up, grad_down], axi...]
    all_gather x2 -> x0, waiting for transfers between devices: 114 us -> none  [the longest x1 65.6 us: body(): lax.all_gather(key_rows, 'seq', axis=1, tiled=True)]
    reduce_scatter x2 -> x0, waiting for transfers between devices: 102 us -> none  [the longest x1 65.4 us: body(): lax.psum_scatter(grad_value.astype(jnp.bfloat16), 'seq', scatter_dimensio...]
    psum x1, waiting for transfers between devices: 196 us -> 98.7 us  [body(): lax.psum(jnp.concatenate([grad_query_w, grad_key_w, grad_value_w, grad_ou...]
    reduce_sum x4 -> x0, other arithmetic: 65.1 us -> none  [forward_block(): row_total = jnp.sum(weights, axis=-1, keepdims=True)]
    pallas_call x0 -> x3, Pallas kernels: none -> 51.2 us  [the longest x1 25.5 us: backward_call(): pl.pallas_call(functools.partial(backward_kernel, blocks // 2), grid_spec...]
  transfers between devices with their start and end apart: 5 -> 15, of which waited for: 5 -> 9; matrix products, arithmetic and copies ran while one was open for 6% -> 8% of each run, Pallas kernels for 0% -> 0%
where the time goes in v1:
time: 647 us; the launch traced here: 650 us
  waiting for transfers between devices  334 us (52%)
  matrix products  97.5 us (15%)
  Pallas kernels  51.2 us (8%)
  blocking collectives  49.6 us (8%)
  starting transfers between devices  38.6 us (6%)
  local copies, waits for them, and re-layouts  38.2 us (6%)
  other arithmetic  26 us (4%)
  between operations  14.9 us (2%)
    ppermute x3, waiting for transfers between devices, body(): own = own + lax.ppermute(total, 'seq', backward).astype(F32)  132 us
    psum x1, waiting for transfers between devices, body(): lax.psum(jnp.concatenate([grad_query_w, grad_key_w, grad_value_w, grad_ou...  98.7 us
    ppermute x3, waiting for transfers between devices, body(): moving = lax.ppermute(moving, 'seq', onward)  97.3 us
    psum x1, blocking collectives, body(): gains = lax.psum(jnp.stack([grad_gain_attn, grad_gain_mlp]), both)  49.6 us
    dot_general x7, matrix products, project_back(): jnp.einsum('rte,de->rtd', gradient, matrix, preferred_element_type=F32)  43 us
    dot_general x4, matrix products, project(): jnp.einsum('rtd,de->rte', vectors, matrix, preferred_element_type=F32)  29.4 us
    pallas_call x1, Pallas kernels, backward_call(): pl.pallas_call(functools.partial(backward_kernel, blocks // 2), grid_spec...  25.5 us
    dot_general x7, matrix products, weight_grad(): jnp.einsum('rtd,rte->de', vectors, gradient, preferred_element_type=F32)  25.1 us
  transfers between devices with their start and end apart: 15, of which 9 were waited for; matrix products, arithmetic and copies ran while one was open for 8% of the time, Pallas kernels for 0%

profile of v1, /device:TPU:0, one launch (start us, length us, event | category | flops | bytes accessed | tf_op | source)
XLA Modules:
  0.0 650.2 jit_solution(7025248190098627158)
XLA Ops:
  7.3 4.5 copy.63.x_ref
  16.3 10.3 %qkv.1 = (bf16[8,576,256]{2,1,0:T(8,128)(2,1)}, bf16[8,384,256]{2,1,0:T(8,128)(2,1)}, bf16[8,256,576]{2,1,0:T(8,128)(2,1)}) custom-call(s32[11]{0:T(128)} %pad_add_fusion.info, bf16[8,256,576]{2,1,0:T(8,128)(2,1)} %copy.63.x_ref, f32[1,576]{1,0:T(1,128)} %broadcast_in_dim.2.gain_ref, bf16[960,576]{1,0:T(8,128)(2,1)} %maximum_bitcast_fusion.w_ref, ...), custom_call_target="tpu_custom_call" | custom-call | tf_op jit(solution)/shard_map/qkv/pallas_call | solution.py:97
  26.6 4.9 collective-permute-start.1
  31.6 33.9 %collective-permute-done.1.refs_2_ = bf16[8,384,256]{2,1,0:T(8,128)(2,1)S(1)} collective-permute-done((bf16[8,384,256]{2,1,0:T(8,128)(2,1)}, bf16[8,384,256]{2,1,0:T(8,128)(2,1)S(1)}, u32[]{:S(2)}, u32[]{:S(2)}) %collective-permute-start.1) | collective-permute-done | bytes 1572896 | tf_op jit(solution)/shard_map/ppermute | solution.py:401
  65.4 4.4 collective-permute-start.3
  69.8 32.7 %collective-permute-done.3.refs_4_ = bf16[8,384,256]{2,1,0:T(8,128)(2,1)S(1)} collective-permute-done((bf16[8,384,256]{2,1,0:T(8,128)(2,1)S(1)}, bf16[8,384,256]{2,1,0:T(8,128)(2,1)S(1)}, u32[]{:S(2)}, u32[]{:S(2)}) %collective-permute-start.3) | collective-permute-done | bytes 1572896 | tf_op jit(solution)/shard_map/ppermute | solution.py:401
  102.5 4.8 collective-permute-start.5
  107.9 30.8 %collective-permute-done.5.refs_6_ = bf16[8,384,256]{2,1,0:T(8,128)(2,1)S(1)} collective-permute-done((bf16[8,384,256]{2,1,0:T(8,128)(2,1)S(1)}, bf16[8,384,256]{2,1,0:T(8,128)(2,1)S(1)}, u32[]{:S(2)}, u32[]{:S(2)}) %collective-permute-start.5) | collective-permute-done | bytes 1572896 | tf_op jit(solution)/shard_map/ppermute | solution.py:401
  138.8 3.3 collective-permute-done.6.refs_7_
  143.3 15.4 %attention_forward.1 = (bf16[8,256,576]{2,1,0:T(8,128)(2,1)}, f32[8,9,256]{2,1,0:T(8,128)}) custom-call(s32[11]{0:T(128)} %pad_add_fusion.info, bf16[8,576,256]{2,1,0:T(8,128)(2,1)} %get-tuple-element.25.q_ref, bf16[8,384,256]{2,1,0:T(8,128)(2,1)} %get-tuple-element.26.refs_0_, bf16[8,384,256]{2,1,0:T(8,128)(2,1)} %copy-done.12, ...), custom_call_target="tpu_custom_call" | custom-call | tf_op jit(solution)/shard_map/attention_forward/pallas_call | solution.py:214
  158.7 4.1 multiply_reduce_fusion.2
  163.4 1.7 copy-done.6
  165.7 8.6 %fusion.18 = f32[8,256,1536]{2,1,0:T(8,128)} fusion(bf16[8,256,576]{1,2,0:T(8,128)(2,1)S(1)} %multiply_convert_fusion.4, bf16[576,1536]{1,0:T(8,128)(2,1)S(1)} %copy-done.37), kind=kOutput, calls=%fused_computation.42 | convolution fusion | flops 3623878656 | bytes 16711680 | tf_op jit(solution)/shard_map/rtd,de->rte/dot_general | solution.py:44
  174.3 8.0 %fusion.22 = f32[8,256,1536]{2,1,0:T(8,128)} fusion(bf16[8,256,576]{1,2,0:T(8,128)(2,1)S(1)} %multiply_convert_fusion.4, bf16[576,1536]{1,0:T(8,128)(2,1)S(1)} %copy-done.36), kind=kOutput, calls=%fused_computation.46 | convolution fusion | flops 3623878656 | bytes 16711680 | tf_op jit(solution)/shard_map/rtd,de->rte/dot_general | solution.py:44
  182.3 21.9 %multiply_convert_fusion = (bf16[8,256,1536]{2,1,0:T(8,128)(2,1)}, bf16[8,256,1536]{2,1,0:T(8,128)(2,1)}, bf16[8,256,1536]{2,1,0:T(8,128)(2,1)}) fusion(f32[8,256,1536]{2,1,0:T(8,128)} %fusion.22, f32[8,256,1536]{2,1,0:T(8,128)} %fusion.18, bf16[1536,576]{0,1:T(8,128)(2,1)S(1)} %copy-done, bf16[8,256,576]{1,2,0:T(8,128)(2,1)} %param.23, ...), kind=kOutput, calls=%fused_computation | convolution fusion | flops 3674603520 | bytes 48177152 | tf_op jit(solution)/shard_map/rte,de->rtd/dot_general | solution.py:48
  204.3 6.6 %fusion.20 = f32[8,256,576]{1,2,0:T(8,128)S(1)} fusion(bf16[8,256,1536]{2,1,0:T(8,128)(2,1)} %get-tuple-element.81, bf16[576,1536]{1,0:T(8,128)(2,1)} %param.20), kind=kOutput, calls=%fused_computation.44 | convolution fusion | flops 3623878656 | bytes 12779520 | tf_op jit(solution)/shard_map/rte,de->rtd/dot_general | solution.py:48
  211.4 4.4 multiply_reduce_fusion
  217.1 2.1 copy-done.5
  219.3 3.4 convolution_convert_fusion
  222.7 4.3 copy.66.dmix_ref
  227.0 25.5 %attention_backward.1 = (bf16[8,256,576]{2,1,0:T(8,128)(2,1)}, bf16[8,256,384]{2,1,0:T(8,128)(2,1)}, bf16[8,256,384]{2,1,0:T(8,128)(2,1)}, bf16[8,256,384]{2,1,0...) custom-call(s32[11]{0:T(128)} %pad_add_fusion.info, ...), custom_call_target="tpu_custom_call" | custom-call | tf_op jit(solution)/shard_map/attention_backward/pallas_call | solution.py:322
  252.6 18.4 %collective-permute-start.10 = (bf16[8,256,384]{2,1,0:T(8,128)(2,1)}, bf16[8,256,384]{2,1,0:T(8,128)(2,1)S(1)}, u32[]{:S(2)}, u32[]{:S(2)}) collective-permute-start(bf16[8,256,384]{2,1,0:T(8,128)(2,1)} %get-tuple-element.37), channel_id=1, source_target_pairs={{0,1},{1,0},{2,3},{3,2},{4,5},{5,4},{6,7},{7,6},{8,9},{9,8},{10,11... | collective-permute-start | bytes 4718600 | tf_op jit(solution)/shard_map/ppermute | solution.py:438
  271.0 3.2 collective-permute-done.10
  274.2 2.0 add_convert_fusion.3
  279.1 6.7 %bitcast_convert_fusion.1 = bf16[576,1536]{1,0:T(8,128)(2,1)S(1)} fusion(bf16[8,256,576]{1,2,0:T(8,128)(2,1)S(1)} %copy-done.24, bf16[8,256,1536]{2,1,0:T(8,128)(2,1)} %get-tuple-element.80), kind=kOutput, calls=%fused_computation.30 | convolution fusion | flops 3624763392 | bytes 10420224 | tf_op jit(solution)/shard_map/rtd,rte->de/dot_general | solution.py:52
  285.8 67.0 %collective-permute-done.11 = bf16[8,256,384]{2,1,0:T(8,128)(2,1)S(1)} collective-permute-done((bf16[8,256,384]{2,1,0:T(8,128)(2,1)S(1)}, bf16[8,256,384]{2,1,0:T(8,128)(2,1)S(1)}, u32[]{:S(2)}, u32[]{:S(2)}) %collective-permute-start.11) | collective-permute-done | bytes 1572896 | tf_op jit(solution)/shard_map/ppermute | solution.py:442
  355.1 2.9 bitcast_convert_fusion.4
  358.1 3.1 bitcast_convert_fusion.3
  361.2 3.8 bitcast_convert_fusion
  365.1 35.4 %collective-permute-done.12 = bf16[8,256,384]{2,1,0:T(8,128)(2,1)S(1)} collective-permute-done((bf16[8,256,384]{2,1,0:T(8,128)(2,1)S(1)}, bf16[8,256,384]{2,1,0:T(8,128)(2,1)S(1)}, u32[]{:S(2)}, u32[]{:S(2)}) %collective-permute-start.12) | collective-permute-done | bytes 1572896 | tf_op jit(solution)/shard_map/ppermute | solution.py:442
  401.2 1.7 collective-permute-start.13
  402.9 3.8 bitcast_convert_fusion.2
  406.7 2.7 pad_maximum_fusion
  409.4 29.2 %collective-permute-done.13 = bf16[8,256,384]{2,1,0:T(8,128)(2,1)S(1)} collective-permute-done((bf16[8,256,384]{2,1,0:T(8,128)(2,1)S(1)}, bf16[8,256,384]{2,1,0:T(8,128)(2,1)S(1)}, u32[]{:S(2)}, u32[]{:S(2)}) %collective-permute-start.13) | collective-permute-done | bytes 1572896 | tf_op jit(solution)/shard_map/ppermute | solution.py:442
  440.9 1.7 fusion.28
  444.6 1.8 copy.74
  446.4 3.2 fusion.25
  449.7 1.8 copy.75
  451.5 4.1 concatenate.21
  455.6 8.6 %multiply_convert_fusion.3 = bf16[8,256,576]{1,2,0:T(8,128)(2,1)} fusion(f32[8,256,576]{1,2,0:T(8,128)} %copy-done.6, f32[8,256]{1,0:T(8,128)S(1)} %compare_convert_fusion, bf16[8,256,1536]{2,1,0:T(8,128)(2,1)} %get-tuple-element.82, bf16[1536,576]{0,1:T(8,128)(2,1)S(1)} %copy-done), kind=kOutput, calls=%fused_computation.25 | convolution fusion | flops 3627417600 | bytes 15147008 | tf_op jit(solution)/shard_map/rtd,de->rte/dot_general | solution.py:44
  467.9 4.9 fusion.9
  472.8 49.6 %psum.21 = f32[2,576]{1,0:T(2,128)S(1)} all-reduce(f32[2,576]{1,0:T(2,128)S(1)} %pad_maximum_fusion.3), channel_id=1, replica_groups=mesh['batch'=4,'seq'=8] {'batch','seq'}, use_global_device_ids=true, to_apply=%region_6.7 | all-reduce | flops 1152 | bytes 9216 | tf_op jit(solution)/shard_map/psum | solution.py:478
  523.1 7.1 %fusion.8 = bf16[8,256,576]{1,2,0:T(8,128)(2,1)} fusion(f32[8,256,576]{1,2,0:T(8,128)} %copy-done.5, bf16[8,256,576]{1,2,0:T(8,128)(2,1)} %param.12, f32[8,256,576]{1,2,0:T(8,128)} %get-tuple-element.100, f32[8,256]{1,0:T(8,128)S(1)} %broadcast_multiply_fusion, f32[576]{0:T(1024)S(1)} %copy-done.31, f32[8,256]{1,0:T(8,128)S(1)} %add_rsqrt_fusion), kind=kLoop, calls=%fused_computation.16 | loop fusion | flops 9437184 | bytes 14174464 | tf_op jit(solution)/shard_map/convert_element_type | solution.py:466
  530.1 98.7 %all-reduce.3.cloned.1.call-done = (bf16[576,1536]{1,0:T(8,128)(2,1)}, bf16[576,4608]{1,0:T(8,128)(2,1)}) async-done(((bf16[576,1536]{1,0:T(8,128)(2,1)}, bf16[576,4608]{1,0:T(8,128)(2,1)}), (bf16[576,1536]{1,0:T(8,128)(2,1)}, bf16[576,4608]{1,0:T(8,128)(2,1)})) %all-reduce.3.cloned.1.call-update) | async-done | bytes 7077904 | tf_op jit(solution)/shard_map/psum | solution.py:472
  628.9 4.1 convert_element_type.144
  633.0 3.9 fusion.37
  636.9 2.0 fusion.38
  639.1 2.0 slice_bitcast_fusion
  (149 shorter events, 25.9 us)
Async XLA Ops:
  7.2 175.1 %copy-start = (bf16[1536,576]{0,1:T(8,128)(2,1)S(1)}, bf16[1536,576]{0,1:T(8,128)(2,1)}, u32[]{:S(2)}) copy-start(bf16[1536,576]{0,1:T(8,128)(2,1)} %param.22) | copy-start | bytes 5308420
  7.2 4.6 copy-start.16
  7.2 621.7 %all-reduce.3.cloned.1.call-start = ((), (), s32[]{:S(2)}) async-start(), calls=%async_computation | async-start | bytes 14155776 | tf_op jit(solution)/shard_map/psum | solution.py:472
  7.3 4.9 copy-start.31
  7.3 6.3 copy-start.28
  26.6 38.8 %collective-permute-start.1 = (bf16[8,384,256]{2,1,0:T(8,128)(2,1)}, bf16[8,384,256]{2,1,0:T(8,128)(2,1)S(1)}, u32[]{:S(2)}, u32[]{:S(2)}) collective-permute-start(bf16[8,384,256]{2,1,0:T(8,128)(2,1)} %get-tuple-element.26.refs_0_), channel_id=1, source_target_pairs={{0,2},{1,3},{2,4},{3,5},{4,6},{5,7},{8,10},{9,11},{10,12},{11,13},... | collective-permute-start | bytes 4718600 | tf_op jit(solution)/shard_map/ppermute | solution.py:401
  65.4 77.9 %copy-start.9 = (bf16[8,384,256]{2,1,0:T(8,128)(2,1)}, bf16[8,384,256]{2,1,0:T(8,128)(2,1)S(1)}, u32[]{:S(2)}) copy-start(bf16[8,384,256]{2,1,0:T(8,128)(2,1)S(1)} %collective-permute-done.1.refs_2_) | copy-start | bytes 4718596
  65.4 37.0 %collective-permute-start.3 = (bf16[8,384,256]{2,1,0:T(8,128)(2,1)S(1)}, bf16[8,384,256]{2,1,0:T(8,128)(2,1)S(1)}, u32[]{:S(2)}, u32[]{:S(2)}) collective-permute-start(bf16[8,384,256]{2,1,0:T(8,128)(2,1)S(1)} %collective-permute-done.1.refs_2_), channel_id=1, source_target_pairs={{0,2},{1,3},{2,4},{3,5},{4,6},{5,7},{8,10},{9,11},{10,12},{11,13},... | collective-permute-start | bytes 4718600 | tf_op jit(solution)/shard_map/ppermute | solution.py:401
  102.5 40.8 %copy-start.10 = (bf16[8,384,256]{2,1,0:T(8,128)(2,1)}, bf16[8,384,256]{2,1,0:T(8,128)(2,1)S(1)}, u32[]{:S(2)}) copy-start(bf16[8,384,256]{2,1,0:T(8,128)(2,1)S(1)} %collective-permute-done.3.refs_4_) | copy-start | bytes 4718596
  102.5 36.2 %collective-permute-start.5 = (bf16[8,384,256]{2,1,0:T(8,128)(2,1)S(1)}, bf16[8,384,256]{2,1,0:T(8,128)(2,1)S(1)}, u32[]{:S(2)}, u32[]{:S(2)}) collective-permute-start(bf16[8,384,256]{2,1,0:T(8,128)(2,1)S(1)} %collective-permute-done.3.refs_4_), channel_id=1, source_target_pairs={{0,2},{1,3},{2,4},{3,5},{4,6},{5,7},{8,10},{9,11},{10,12},{11,13},... | collective-permute-start | bytes 4718600 | tf_op jit(solution)/shard_map/ppermute | solution.py:401
  107.3 31.5 %collective-permute-start = (bf16[8,384,256]{2,1,0:T(8,128)(2,1)}, bf16[8,384,256]{2,1,0:T(8,128)(2,1)S(1)}, u32[]{:S(2)}, u32[]{:S(2)}) collective-permute-start(bf16[8,384,256]{2,1,0:T(8,128)(2,1)} %get-tuple-element.26.refs_0_), channel_id=1, source_target_pairs={{0,1},{1,0},{2,3},{3,2},{4,5},{5,4},{6,7},{7,6},{8,9},{9,8},{10,11... | collective-permute-start | bytes 4718600 | tf_op jit(solution)/shard_map/ppermute | solution.py:402
  107.3 31.5 %collective-permute-start.2 = (bf16[8,384,256]{2,1,0:T(8,128)(2,1)S(1)}, bf16[8,384,256]{2,1,0:T(8,128)(2,1)S(1)}, u32[]{:S(2)}, u32[]{:S(2)}) collective-permute-start(bf16[8,384,256]{2,1,0:T(8,128)(2,1)S(1)} %collective-permute-done.1.refs_2_), channel_id=1, source_target_pairs={{0,1},{1,0},{2,3},{3,2},{4,5},{5,4},{6,7},{7,6},{8,9},{9,8},{10,11... | collective-permute-start | bytes 4718600 | tf_op jit(solution)/shard_map/ppermute | solution.py:402
  107.8 31.0 %collective-permute-start.4 = (bf16[8,384,256]{2,1,0:T(8,128)(2,1)S(1)}, bf16[8,384,256]{2,1,0:T(8,128)(2,1)S(1)}, u32[]{:S(2)}, u32[]{:S(2)}) collective-permute-start(bf16[8,384,256]{2,1,0:T(8,128)(2,1)S(1)} %collective-permute-done.3.refs_4_), channel_id=1, source_target_pairs={{0,1},{1,0},{2,3},{3,2},{4,5},{5,4},{6,7},{7,6},{8,9},{9,8},{10,11... | collective-permute-start | bytes 4718600 | tf_op jit(solution)/shard_map/ppermute | solution.py:402
  138.7 3.4 collective-permute-start.6
  143.3 15.4 %copy-start.1 = (bf16[8,256,576]{1,2,0:T(8,128)(2,1)S(1)}, bf16[8,256,576]{1,2,0:T(8,128)(2,1)}, u32[]{:S(2)}) copy-start(bf16[8,256,576]{1,2,0:T(8,128)(2,1)} %param.12) | copy-start | bytes 7077892
  143.3 15.4 %copy-start.40 = (bf16[576,576]{1,0:T(8,128)(2,1)S(1)}, bf16[576,576]{1,0:T(8,128)(2,1)}, u32[]{:S(2)}) copy-start(bf16[576,576]{1,0:T(8,128)(2,1)} %param.18) | copy-start | bytes 1990660
  158.7 4.2 copy-start.32
  165.7 8.6 %copy-start.23 = (bf16[8,256,576]{1,2,0:T(8,128)(2,1)}, bf16[8,256,576]{1,2,0:T(8,128)(2,1)S(1)}, u32[]{:S(2)}) copy-start(bf16[8,256,576]{1,2,0:T(8,128)(2,1)S(1)} %multiply_convert_fusion.4) | copy-start | bytes 7077892
  165.7 8.6 %copy-start.36 = (bf16[576,1536]{1,0:T(8,128)(2,1)S(1)}, bf16[576,1536]{1,0:T(8,128)(2,1)}, u32[]{:S(2)}) copy-start(bf16[576,1536]{1,0:T(8,128)(2,1)} %param.20) | copy-start | bytes 5308420
  204.2 6.7 %copy-start.7 = (f32[8,256,576]{1,2,0:T(8,128)S(1)}, f32[8,256,576]{1,2,0:T(8,128)}, u32[]{:S(2)}) copy-start(f32[8,256,576]{1,2,0:T(8,128)} %copy-done.6) | copy-start | bytes 14155780
  204.3 6.7 %copy-start.38 = (bf16[576,1536]{1,0:T(8,128)(2,1)S(1)}, bf16[576,1536]{1,0:T(8,128)(2,1)}, u32[]{:S(2)}) copy-start(bf16[576,1536]{1,0:T(8,128)(2,1)} %param.21) | copy-start | bytes 5308420
  204.3 7.1 %copy-start.42 = (bf16[8,256,1536]{2,1,0:T(8,128)(2,1)S(1)}, bf16[8,256,1536]{2,1,0:T(8,128)(2,1)}, u32[]{:S(2)}) copy-start(bf16[8,256,1536]{2,1,0:T(8,128)(2,1)} %get-tuple-element.80) | copy-start | bytes 18874372
  211.4 4.4 copy-start.21
  252.6 25.2 %copy-start.2 = (bf16[8,256,576]{1,2,0:T(8,128)(2,1)S(1)}, bf16[8,256,576]{1,2,0:T(8,128)(2,1)}, u32[]{:S(2)}) copy-start(bf16[8,256,576]{1,2,0:T(8,128)(2,1)} %param.12) | copy-start | bytes 7077892
  252.6 21.6 %collective-permute-start.10 = (bf16[8,256,384]{2,1,0:T(8,128)(2,1)}, bf16[8,256,384]{2,1,0:T(8,128)(2,1)S(1)}, u32[]{:S(2)}, u32[]{:S(2)}) collective-permute-start(bf16[8,256,384]{2,1,0:T(8,128)(2,1)} %get-tuple-element.37), channel_id=1, source_target_pairs={{0,1},{1,0},{2,3},{3,2},{4,5},{5,4},{6,7},{7,6},{8,9},{9,8},{10,11... | collective-permute-start | bytes 4718600 | tf_op jit(solution)/shard_map/ppermute | solution.py:438
  271.0 14.9 %collective-permute-start.9 = (bf16[8,256,384]{2,1,0:T(8,128)(2,1)}, bf16[8,256,384]{2,1,0:T(8,128)(2,1)S(1)}, u32[]{:S(2)}, u32[]{:S(2)}) collective-permute-start(bf16[8,256,384]{2,1,0:T(8,128)(2,1)} %get-tuple-element.35), channel_id=1, source_target_pairs={{0,1},{1,0},{2,3},{3,2},{4,5},{5,4},{6,7},{7,6},{8,9},{9,8},{10,11... | collective-permute-start | bytes 4718600 | tf_op jit(solution)/shard_map/ppermute | solution.py:438
  274.2 4.7 copy-start.39
  274.2 4.8 copy-start.24
  274.2 87.0 %slice-start.4 = ((s8[6291456]{0:T(1024)(128)(4,1)}), s8[4194304]{0:T(1024)(128)(4,1)S(1)}, s32[]{:S(2)}) async-start(s8[6291456]{0:T(1024)(128)(4,1)} %bitcast.111), calls=%async_computation.5 | async-start | bytes 8388608
  276.2 76.6 %collective-permute-start.11 = (bf16[8,256,384]{2,1,0:T(8,128)(2,1)S(1)}, bf16[8,256,384]{2,1,0:T(8,128)(2,1)S(1)}, u32[]{:S(2)}, u32[]{:S(2)}) collective-permute-start(bf16[8,256,384]{2,1,0:T(8,128)(2,1)S(1)} %add_convert_fusion.3), channel_id=1, source_target_pairs={{2,0},{3,1},{4,2},{5,3},{6,4},{7,5},{10,8},{11,9},{12,10},{13,11},... | collective-permute-start | bytes 4718600 | tf_op jit(solution)/shard_map/ppermute | solution.py:442
  278.5 86.6 %collective-permute-start.8 = (bf16[8,256,384]{2,1,0:T(8,128)(2,1)}, bf16[8,256,384]{2,1,0:T(8,128)(2,1)S(1)}, u32[]{:S(2)}, u32[]{:S(2)}) collective-permute-start(bf16[8,256,384]{2,1,0:T(8,128)(2,1)} %get-tuple-element.33), channel_id=1, source_target_pairs={{0,1},{1,0},{2,3},{3,2},{4,5},{5,4},{6,7},{7,6},{8,9},{9,8},{10,11... | collective-permute-start | bytes 4718600 | tf_op jit(solution)/shard_map/ppermute | solution.py:438
  278.9 73.9 %copy-start.27 = (bf16[8,256,384]{2,1,0:T(8,128)(2,1)S(1)}, bf16[8,256,384]{2,1,0:T(8,128)(2,1)}, u32[]{:S(2)}) copy-start(bf16[8,256,384]{2,1,0:T(8,128)(2,1)} %get-tuple-element.34) | copy-start | bytes 4718596
  278.9 82.3 %slice-start.5 = ((s8[6291456]{0:T(1024)(128)(4,1)}), s8[2097152]{0:T(1024)(128)(4,1)S(1)}, s32[]{:S(2)}) async-start(s8[6291456]{0:T(1024)(128)(4,1)} %bitcast.111), calls=%async_computation.6 | async-start | bytes 4194304
  278.9 130.5 %collective-permute-start.7 = (bf16[8,256,384]{2,1,0:T(8,128)(2,1)S(1)}, bf16[8,256,384]{2,1,0:T(8,128)(2,1)S(1)}, u32[]{:S(2)}, u32[]{:S(2)}) collective-permute-start(bf16[8,256,384]{2,1,0:T(8,128)(2,1)S(1)} %copy-done.39), channel_id=1, source_target_pairs={{0,1},{1,0},{2,3},{3,2},{4,5},{5,4},{6,7},{7,6},{8,9},{9,8},{10,11... | collective-permute-start | bytes 4718600 | tf_op jit(solution)/shard_map/ppermute | solution.py:438
  279.1 76.0 %copy-start.18 = (bf16[8,256,576]{2,1,0:T(8,128)(2,1)S(1)}, bf16[8,256,576]{2,1,0:T(8,128)(2,1)}, u32[]{:S(2)}) copy-start(bf16[8,256,576]{2,1,0:T(8,128)(2,1)} %get-tuple-element.29) | copy-start | bytes 7077892
  279.1 76.0 %copy-start.34 = (bf16[8,256,576]{2,1,0:T(8,128)(2,1)S(1)}, bf16[8,256,576]{2,1,0:T(8,128)(2,1)}, u32[]{:S(2)}) copy-start(bf16[8,256,576]{2,1,0:T(8,128)(2,1)} %get-tuple-element.38) | copy-start | bytes 7077892
  352.8 5.2 slice-start
  352.8 5.2 slice-start.1
  353.5 4.5 copy-start.20
  353.5 47.0 %collective-permute-start.12 = (bf16[8,256,384]{2,1,0:T(8,128)(2,1)S(1)}, bf16[8,256,384]{2,1,0:T(8,128)(2,1)S(1)}, u32[]{:S(2)}, u32[]{:S(2)}) collective-permute-start(bf16[8,256,384]{2,1,0:T(8,128)(2,1)S(1)} %add_convert_fusion.2), channel_id=1, source_target_pairs={{2,0},{3,1},{4,2},{5,3},{6,4},{7,5},{10,8},{11,9},{12,10},{13,11},... | collective-permute-start | bytes 4718600 | tf_op jit(solution)/shard_map/ppermute | solution.py:442
  358.1 44.8 %slice-start.2 = ((s8[6291456]{0:T(1024)(128)(4,1)}), s8[4194304]{0:T(1024)(128)(4,1)S(1)}, s32[]{:S(2)}) async-start(s8[6291456]{0:T(1024)(128)(4,1)} %bitcast.109), calls=%async_computation.3 | async-start | bytes 8388608
  361.2 39.3 %copy-start.26 = (bf16[8,256,384]{2,1,0:T(8,128)(2,1)S(1)}, bf16[8,256,384]{2,1,0:T(8,128)(2,1)}, u32[]{:S(2)}) copy-start(bf16[8,256,384]{2,1,0:T(8,128)(2,1)} %get-tuple-element.32) | copy-start | bytes 4718596
  361.2 41.7 %slice-start.3 = ((s8[6291456]{0:T(1024)(128)(4,1)}), s8[2097152]{0:T(1024)(128)(4,1)S(1)}, s32[]{:S(2)}) async-start(s8[6291456]{0:T(1024)(128)(4,1)} %bitcast.109), calls=%async_computation.4 | async-start | bytes 4194304
  401.2 37.4 %collective-permute-start.13 = (bf16[8,256,384]{2,1,0:T(8,128)(2,1)S(1)}, bf16[8,256,384]{2,1,0:T(8,128)(2,1)S(1)}, u32[]{:S(2)}, u32[]{:S(2)}) collective-permute-start(bf16[8,256,384]{2,1,0:T(8,128)(2,1)S(1)} %add_convert_fusion.1), channel_id=1, source_target_pairs={{2,0},{3,1},{4,2},{5,3},{6,4},{7,5},{10,8},{11,9},{12,10},{13,11},... | collective-permute-start | bytes 4718600 | tf_op jit(solution)/shard_map/ppermute | solution.py:442
  406.7 31.9 %copy-start.25 = (bf16[8,256,384]{2,1,0:T(8,128)(2,1)S(1)}, bf16[8,256,384]{2,1,0:T(8,128)(2,1)}, u32[]{:S(2)}) copy-start(bf16[8,256,384]{2,1,0:T(8,128)(2,1)} %get-tuple-element.30) | copy-start | bytes 4718596
  455.6 8.7 %copy-start.29 = (bf16[576,192]{0,1:T(8,128)(2,1)S(1)}, bf16[576,192]{0,1:T(8,128)(2,1)}, u32[]{:S(2)}) copy-start(bf16[576,192]{0,1:T(8,128)(2,1)} %param.16) | copy-start | bytes 663556
  628.9 4.1 copy-start.4
  633.0 4.0 copy-start.8
  (16 other events, 41.7 us)
Sparse Core Ops, SparseCore 0:
  455.7 173.0 all-reduce.2
